TPU v7x, 256 devices: a whole 4x4x8 slice. The times are simulated.
256 devices in a mesh: gx: 8 (over y, core), gy: 8 (over z_lo, x), gz: 4 (over z_hi).
Axes of the slice: x: 4, y: 4, z: 8 (z_hi: 4, z_lo: 2; z = z_hi * 2 + z_lo), core: 2. Of those that a mesh axis runs over, the one named last changes fastest.
Arguments:
- latent: float32 [65536, 128], P(('gx', 'gy', 'gz')), may hold values from -6 to 6
- position: float32 [3, 65536], P(None, ('gx', 'gy', 'gz')), may hold values from 0 to 8, as said below
- particle_count: int32 [256], P(('gx', 'gy', 'gz')), may hold values from 64 to 256, as said below
- nbr_count: int32 [65536], P(('gx', 'gy', 'gz')), may hold values from 1 to 16, as said below
- senders: int32 [1048576], P(('gx', 'gy', 'gz')), may hold values from 0 to 639, as said below
- ghost_x: int32 [512, 64], P(('gx', 'gy', 'gz')), may hold values from 0 to 255, as said below
- ghost_y: int32 [512, 64], P(('gx', 'gy', 'gz')), may hold values from 0 to 383, as said below
- ghost_z: int32 [512, 64], P(('gx', 'gy', 'gz')), may hold values from 0 to 511, as said below
- w_send: float32 [128, 128], replicated, may hold values from -0.375 to 0.375
- w_recv: float32 [128, 128], replicated, may hold values from -0.375 to 0.375
- w_geo: float32 [4, 128], replicated, may hold values from -1.5 to 1.5
- w_msg: float32 [128, 128], replicated, may hold values from -0.125 to 0.125
- w_dec: float32 [3, 128], replicated, may hold values from -0.5 to 0.5
- cot_latent: float32 [65536, 128], P(('gx', 'gy', 'gz')), may hold values from -6 to 6
- cot_position: float32 [3, 65536], P(None, ('gx', 'gy', 'gz')), may hold values from -6 to 6
Outputs:
- grad_latent: float32 [65536, 128], P(('gx', 'gy', 'gz'))
- grad_position: float32 [3, 65536], P(None, ('gx', 'gy', 'gz'))
- grad_send: float32 [128, 128], replicated
- grad_recv: float32 [128, 128], replicated
- grad_geo: float32 [4, 128], replicated
- grad_msg: float32 [128, 128], replicated
- grad_dec: float32 [3, 128], replicated
Inputs may be any that keep to these rules, and one draw needn't show every extreme that they name: `particle_count`: between 1/4 of the slots and all; some cell is full. `nbr_count`: each particle's first slot is live; every cell has a particle with all 16 slots live. `senders`: a live own row, or a ghost row of the finished table; the last slot of each cell names its last ghost row. `ghost_x`: live own rows; each list's last entry is its cell's last live row. `ghost_y`: live own rows or rows appended along x; each list's last entry is the last such row. `ghost_z`: live own rows or rows appended along x or y; each list's last entry is the last such row. `position`: each particle lies inside its own unit cell.
All inputs are finite; a program needn't handle non-finite values.
Results may differ from a plain program's by a relative error of at most 0.0003.
Values sent between devices are 32-bit elements; how exact they have to be, the bound alone decides.
A program may use at most 192 MiB of HBM per device.

v0:
```python
import math

import jax
import jax.numpy as jnp
from jax import lax
from jax.sharding import PartitionSpec as P

BLOCK = 128


STRIDE = 0.1
PRECISE = lax.Precision.HIGHEST


def padded(shard, sides, width):
    for axis, dim in sides:
        size, length = (lax.axis_size(axis), shard.shape[dim])
        up = [(i, (i + 1) % size) for i in range(size)]
        down = [(j, i) for i, j in up]
        last = lax.slice_in_dim(shard, length - width, length, axis=dim)
        leading = lax.slice_in_dim(shard, 0, width, axis=dim)
        before = lax.ppermute(last, axis, up)
        after = lax.ppermute(leading, axis, down)
        shard = jnp.concatenate([before, shard, after], axis=dim)
    return shard


def matmul(left, right):
    return jnp.dot(left, right, precision=PRECISE, preferred_element_type=jnp.float32)


def selector(rows, total):
    return (rows[..., None] == jnp.arange(total)[None, :]).astype(jnp.float32)


def local_step(table_x, table_p, senders, nbr_count, live, w_send, w_recv, w_geo, w_msg, w_dec):
    parts = live.shape[0]
    slots = senders.shape[0] // parts
    blocks = parts // BLOCK
    table_rows = table_x.shape[0]
    proj_send = matmul(table_x, w_send)
    own_x = table_x[:parts]
    own_p = table_p[:, :parts]
    proj_recv = matmul(own_x, w_recv)

    def one_block(inputs):
        sender_rows, recv_rows, recv_pos, counts = inputs
        picker = selector(sender_rows, table_rows)
        gathered = matmul(picker, proj_send)
        sender_pos = lax.dot_general(
            table_p,
            picker,
            (((1,), (1,)), ((), ())),
            precision=PRECISE,
            preferred_element_type=jnp.float32,
        )
        rel = sender_pos - jnp.repeat(recv_pos, slots, axis=1)
        dist = jnp.sum(rel * rel, axis=0, keepdims=True)
        geo = jnp.concatenate([rel, dist], axis=0)
        geo_term = lax.dot_general(
            geo,
            w_geo,
            (((0,), (0,)), ((), ())),
            precision=PRECISE,
            preferred_element_type=jnp.float32,
        )
        pre = gathered + jnp.repeat(recv_rows, slots, axis=0) + geo_term
        message = matmul(jax.nn.silu(pre), w_msg)
        keep = (jnp.arange(slots)[None, :] < counts[:, None]).astype(message.dtype).reshape(-1, 1)
        return jnp.sum((message * keep).reshape(BLOCK, slots, -1), axis=1)

    pos_blocks = jnp.transpose(own_p.reshape(3, blocks, BLOCK), (1, 0, 2))
    agg = lax.map(
        one_block,
        (
            senders.reshape(blocks, BLOCK * slots),
            proj_recv.reshape(blocks, BLOCK, -1),
            pos_blocks,
            nbr_count.reshape(blocks, BLOCK),
        ),
    )
    new_x = own_x + live[:, None] * agg.reshape(parts, -1)
    move = lax.dot_general(
        w_dec,
        new_x,
        (((1,), (1,)), ((), ())),
        precision=PRECISE,
        preferred_element_type=jnp.float32,
    )
    new_p = own_p + STRIDE * live[None, :] * move
    return (new_x, new_p)


def across_x(joined):
    return padded(joined, (("gx", 0),), 1)


def across_y(joined):
    return padded(joined, (("gy", 0),), 1)


def across_z(joined):
    return padded(joined, (("gz", 0),), 1)


def pack_grads(grads):
    return jnp.concatenate([piece.reshape(-1) for piece in grads])


def unpack_grads(flat, like):
    result = []
    offset = 0
    for piece in like:
        length = piece.size
        result.append(flat[offset : offset + length].reshape(piece.shape))
        offset = offset + length
    return tuple(result)


def reduce_grads(grads):
    return unpack_grads(lax.psum(pack_grads(grads), ("gx", "gy", "gz")), grads)


def grow_table(table_x, table_p, chosen, component, index, count, across):
    width = table_x.shape[1]
    picker = selector(chosen, table_x.shape[0])
    send_x = jnp.einsum(
        "sgr,rw->sgw", picker, table_x, precision=PRECISE, preferred_element_type=jnp.float32
    )
    send_p = jnp.einsum(
        "sgr,cr->sgc", picker, table_p, precision=PRECISE, preferred_element_type=jnp.float32
    )
    lower = count * (index == 0).astype(jnp.float32)
    upper = -count * (index == count - 1).astype(jnp.float32)
    hot = (jnp.arange(3) == component).astype(jnp.float32)
    send_p = send_p + jnp.stack([lower, upper])[:, None, None] * hot[None, None, :]
    got = across(jnp.concatenate([send_x, send_p], axis=2))
    table_x = jnp.concatenate([table_x, got[0, :, :width], got[3, :, :width]], axis=0)
    table_p = jnp.concatenate([table_p, got[0, :, width:].T, got[3, :, width:].T], axis=1)
    return (table_x, table_p)


def shrink_table(cot_x, cot_p, chosen, across):
    count = chosen.shape[1]
    width = cot_x.shape[1]
    rows = cot_x.shape[0] - 2 * count
    back_x = jnp.stack([cot_x[rows : rows + count], cot_x[rows + count :]])
    back_p = jnp.stack([cot_p[:, rows : rows + count].T, cot_p[:, rows + count :].T])
    got = across(jnp.concatenate([back_x, back_p], axis=2))
    arrived = jnp.stack([got[0], got[3]])
    picker = selector(chosen, rows)
    added_x = jnp.einsum(
        "sgr,sgw->rw",
        picker,
        arrived[:, :, :width],
        precision=PRECISE,
        preferred_element_type=jnp.float32,
    )
    added_p = jnp.einsum(
        "sgr,sgc->cr",
        picker,
        arrived[:, :, width:],
        precision=PRECISE,
        preferred_element_type=jnp.float32,
    )
    return (cot_x[:rows] + added_x, cot_p[:, :rows] + added_p)


def per_device(
    latent,
    position,
    particle_count,
    nbr_count,
    senders,
    ghost_x,
    ghost_y,
    ghost_z,
    w_send,
    w_recv,
    w_geo,
    w_msg,
    w_dec,
    cot_latent,
    cot_position,
):
    parts = latent.shape[0]
    live = (jnp.arange(parts) < particle_count[0]).astype(jnp.float32)
    weights = (w_send, w_recv, w_geo, w_msg, w_dec)
    sections = (
        (ghost_x, 0, lax.axis_index("gx"), lax.axis_size("gx"), across_x),
        (ghost_y, 1, lax.axis_index("gy"), lax.axis_size("gy"), across_y),
        (ghost_z, 2, lax.axis_index("gz"), lax.axis_size("gz"), across_z),
    )
    total = lax.axis_size("gx") * lax.axis_size("gy") * lax.axis_size("gz") * parts
    scale = 1.0 / math.sqrt(total)

    def build(field_x, field_p):
        for chosen, component, index, count, across in sections:
            field_x, field_p = grow_table(field_x, field_p, chosen, component, index, count, across)
        return (field_x, field_p)

    def unbuild(cot_x, cot_p):
        for chosen, component, index, count, across in sections[::-1]:
            cot_x, cot_p = shrink_table(cot_x, cot_p, chosen, across)
        return (cot_x, cot_p)

    def step_back(table_x, table_p, cot_x, cot_p):
        outputs, pull = jax.vjp(
            lambda tx, tp, ws: local_step(tx, tp, senders, nbr_count, live, *ws),
            table_x,
            table_p,
            weights,
        )
        return pull((cot_x, cot_p))

    first_x, first_p = build(latent, position)
    latent_one, position_one = local_step(first_x, first_p, senders, nbr_count, live, *weights)
    second_x, second_p = build(latent_one, position_one)
    cot_tx, cot_tp, grads_two = step_back(second_x, second_p, cot_latent, cot_position)
    cot_one_x, cot_one_p = unbuild(cot_tx, cot_tp)
    summed_two = reduce_grads(grads_two)
    cot_tx, cot_tp, grads_one = step_back(first_x, first_p, cot_one_x, cot_one_p)
    grad_latent, grad_position = unbuild(cot_tx, cot_tp)
    summed_one = reduce_grads(grads_one)
    summed = tuple((first + second for first, second in zip(summed_one, summed_two)))
    return (
        grad_latent,
        grad_position,
        summed[0] * scale,
        summed[1] * scale,
        summed[2] * scale,
        summed[3] * scale,
        summed[4] * scale,
    )


def solution(mesh):
    placed = (
        P(("gx", "gy", "gz"), None),
        P(None, ("gx", "gy", "gz")),
        P(("gx", "gy", "gz")),
        P(("gx", "gy", "gz")),
        P(("gx", "gy", "gz")),
        P(("gx", "gy", "gz"), None),
        P(("gx", "gy", "gz"), None),
        P(("gx", "gy", "gz"), None),
        P(),
        P(),
        P(),
        P(),
        P(),
        P(("gx", "gy", "gz"), None),
        P(None, ("gx", "gy", "gz")),
    )
    return jax.shard_map(
        per_device,
        mesh=mesh,
        in_specs=placed,
        out_specs=(
            P(("gx", "gy", "gz"), None),
            P(None, ("gx", "gy", "gz")),
            P(),
            P(),
            P(),
            P(),
            P(),
        ),
        check_vma=False,
    )
```

profile of v0, /device:TPU:1, one launch (start us, length us, event | category | flops | bytes accessed | tf_op | source)
XLA Modules:
  0.0 625.2 jit_solution(8683823611632184103)
XLA Ops:
  9.6 2.7 collective-permute-start
  19.6 2.7 collective-permute-start.3
  24.9 3.1 collective-permute-start.4
  28.2 3.2 collective-permute-start.5
  32.5 2.6 collective-permute-done.5
  36.1 19.2 %while.116 = (s32[]{:T(128)}, f32[2,128,128]{2,1,0:T(8,128)S(1)}, s32[2,2048]{1,0:T(2,128)S(1)}, f32[640,128]{1,0:T(8,128)S(1)}, f32[2,128,128]{2,1,0:T(8,128)S(...) while((s32[]{:T(128)}, f32[2,128,128]{2,1,0:T(8,128)S(1)}, ...), condition=%wide.region_3.4_spmd, body=%wide.region_0.3_spmd.sunk | while | flops 2480418816 | bytes 7323265 | solution.py:73
  36.4 2.7 multiply_reduce_fusion.6
  41.0 2.5 fusion.353
  43.7 2.0 bitcast_reduce_fusion.10
  46.0 2.7 multiply_reduce_fusion.6
  50.6 2.5 fusion.353
  55.3 4.6 broadcast.318.clone
  65.7 34.0 %while.118 = (s32[]{:T(128)}, f32[2,128,128]{2,1,0:T(8,128)S(1)}, f32[2,2048,640]{2,1,0:T(8,128)}, f32[2,3,2048]{2,1,0:T(4,128)}, f32[2,4,2048]{2,1,0:T(4,128)S(...) while((s32[]{:T(128)}, f32[2,128,128]{2,1,0:T(8,128)S(1)}, ...), condition=%wide.region_15.16_spmd.clone.clone, body=%wide.region_12.15_spmd.clone.clone.sunk | while | flops 2484621312 | bytes 33711868 | solution.py:73
  66.6 2.7 multiply_reduce_fusion.8
  71.2 4.0 bitcast_dynamic-update-slice_fusion.34
  76.7 2.4 bitcast_reduce_fusion.12
  79.7 2.5 convert_dynamic-update-slice_fusion.5
  83.2 2.7 multiply_reduce_fusion.8
  87.9 4.0 bitcast_dynamic-update-slice_fusion.34
  93.4 2.4 bitcast_reduce_fusion.12
  96.4 2.6 convert_dynamic-update-slice_fusion.5
  103.1 3.5 collective-permute-start.6
  108.0 2.3 collective-permute-done.7
  111.6 3.1 collective-permute-start.9
  117.3 4.1 collective-permute-start.10
  123.1 3.6 collective-permute-done.11
  127.3 4.6 broadcast.318
  138.5 32.8 %while.117 = (s32[]{:T(128)}, f32[2,128,128]{2,1,0:T(8,128)S(1)}, f32[2,2048,640]{2,1,0:T(8,128)}, f32[2,3,2048]{2,1,0:T(4,128)}, f32[2,4,2048]{2,1,0:T(4,128)S(...) while((s32[]{:T(128)}, f32[2,128,128]{2,1,0:T(8,128)S(1)}, ...), condition=%wide.region_7.8_spmd.clone.clone, body=%wide.region_4.7_spmd.clone.clone.sunk | while | flops 2484621312 | bytes 33711360 | solution.py:73
  138.8 2.7 multiply_reduce_fusion.7
  143.5 4.2 bitcast_dynamic-update-slice_fusion.30
  149.2 2.4 bitcast_reduce_fusion.11
  152.3 2.6 convert_dynamic-update-slice_fusion.4
  155.3 2.7 multiply_reduce_fusion.7
  159.9 4.1 bitcast_dynamic-update-slice_fusion.30
  165.6 2.4 bitcast_reduce_fusion.11
  168.6 2.5 convert_dynamic-update-slice_fusion.4
  172.6 66.5 %while.119 = (s32[]{:T(128)}, f32[640,128]{1,0:T(8,128)}, f32[3,640]{1,0:T(4,128)}, f32[4,128]{1,0:T(4,128)}, f32[128,128]{1,0:T(8,128)}, /*index=5*/f32[2,128,1...) while((s32[]{:T(128)}, f32[640,128]{1,0:T(8,128)}, ...), condition=%wide.region_11.12_spmd.clone, body=%wide.region_8.11_spmd.clone.sunk | while | flops 2892993024 | bytes 30857936 | solution.py:73
  175.1 3.6 bitcast_reduce_fusion.13
  181.9 5.8 fusion.387
  187.7 10.4 %fusion.386 = f32[640,128]{1,0:T(8,128)S(1)} fusion(f32[2048,128]{1,0:T(8,128)S(1)} %get-tuple-element.2117, f32[2,2048,640]{2,1,0:T(8,128)} %get-tuple-element.2340, s32[]{:T(128)S(6)} %sub.55, f32[640,128]{1,0:T(8,128)S(1)} %copy-done.8, pred[]{:T(512)S(6)} %compare.10), kind=kOutput, calls=%fused_computation.117.clone.1 | convolution fusion | flops 2013429760 | bytes 6946821 | tf_op jit(solution)/shard_map/transpose(jvp())/while/body/eval_jaxpr/dot_general | solution.py:29
  202.0 3.7 convolution_add_fusion.20
  208.0 3.6 bitcast_reduce_fusion.13
  214.9 5.8 fusion.387
  220.6 10.4 %fusion.386 = f32[640,128]{1,0:T(8,128)S(1)} fusion(f32[2048,128]{1,0:T(8,128)S(1)} %get-tuple-element.2117, f32[2,2048,640]{2,1,0:T(8,128)} %get-tuple-element.2340, s32[]{:T(128)S(6)} %sub.55, f32[640,128]{1,0:T(8,128)S(1)} %copy-done.8, pred[]{:T(512)S(6)} %compare.10), kind=kOutput, calls=%fused_computation.117.clone.1 | convolution fusion | flops 2013429760 | bytes 6946821 | tf_op jit(solution)/shard_map/transpose(jvp())/while/body/eval_jaxpr/dot_general | solution.py:29
  235.0 3.7 convolution_add_fusion.20
  239.1 2.5 fusion.109
  247.8 2.3 collective-permute-start.13
  255.1 3.5 collective-permute-start.15
  260.8 5.5 collective-permute-start.16
  268.2 3.4 collective-permute-done.17
  274.6 63.2 %while.120 = (s32[]{:T(128)}, f32[640,128]{1,0:T(8,128)}, f32[3,640]{1,0:T(4,128)}, f32[4,128]{1,0:T(4,128)S(1)}, f32[128,128]{1,0:T(8,128)}, /*index=5*/f32[2,1...) while((s32[]{:T(128)}, f32[640,128]{1,0:T(8,128)}, ...), condition=%wide.region_19.20_spmd.clone, body=%wide.region_16.19_spmd.clone.sunk | while | flops 2892993024 | bytes 30448196 | solution.py:73
  277.7 3.6 bitcast_reduce_fusion.14
  284.6 5.8 fusion.402
  290.3 10.4 %fusion.401 = f32[640,128]{1,0:T(8,128)S(1)} fusion(f32[2048,128]{1,0:T(8,128)S(1)} %get-tuple-element.2139, f32[2,2048,640]{2,1,0:T(8,128)} %get-tuple-element.2406, s32[]{:T(128)S(6)} %sub.56, f32[640,128]{1,0:T(8,128)S(1)} %copy-done.5, pred[]{:T(512)S(6)} %compare.11), kind=kOutput, calls=%fused_computation.150.clone.1 | convolution fusion | flops 2013429760 | bytes 6946821 | tf_op jit(solution)/shard_map/transpose(jvp())/while/body/eval_jaxpr/dot_general | solution.py:29
  303.3 2.5 convolution_add_fusion.22
  308.7 3.7 bitcast_reduce_fusion.14
  315.6 5.8 fusion.402
  321.4 10.4 %fusion.401 = f32[640,128]{1,0:T(8,128)S(1)} fusion(f32[2048,128]{1,0:T(8,128)S(1)} %get-tuple-element.2139, f32[2,2048,640]{2,1,0:T(8,128)} %get-tuple-element.2406, s32[]{:T(128)S(6)} %sub.56, f32[640,128]{1,0:T(8,128)S(1)} %copy-done.5, pred[]{:T(512)S(6)} %compare.11), kind=kOutput, calls=%fused_computation.150.clone.1 | convolution fusion | flops 2013429760 | bytes 6946821 | tf_op jit(solution)/shard_map/transpose(jvp())/while/body/eval_jaxpr/dot_general | solution.py:29
  334.3 3.3 convolution_add_fusion.22
  346.4 2.6 collective-permute-start.19
  354.1 2.6 collective-permute-start.21
  359.0 3.2 collective-permute-start.22
  364.2 3.7 collective-permute-done.23
  370.0 244.0 %all-reduce.7.cloned.1.call-done = (f32[50048]{0:T(1024)}, f32[50048]{0:T(1024)}) async-done(((f32[50048]{0:T(1024)}, f32[50048]{0:T(1024)}), (f32[50048]{0:T(1024)}, f32[50048]{0:T(1024)})) %all-reduce.7.cloned.1.call-update) | async-done | bytes 400400 | tf_op jit(solution)/shard_map/psum | solution.py:121
  (594 shorter events, 141.2 us)
Async XLA Ops:
  7.2 28.2 %copy-start = (f32[128,128]{1,0:T(8,128)S(1)}, f32[128,128]{1,0:T(8,128)}, u32[]{:S(2)}) copy-start(f32[128,128]{1,0:T(8,128)} %param.33) | copy-start | bytes 196612
  7.2 17.3 %copy-start.54 = (f32[3,256]{1,0:T(4,128)S(1)}, f32[3,256]{1,0:T(4,128)}, u32[]{:S(2)}) copy-start(f32[3,256]{1,0:T(4,128)} %param.26) | copy-start | bytes 9220
  7.2 16.9 %copy-start.60 = (s32[2,64]{1,0:T(2,128)S(1)}, s32[2,64]{1,0:T(2,128)}, u32[]{:S(2)}) copy-start(s32[2,64]{1,0:T(2,128)} %param.32) | copy-start | bytes 1540
  7.2 20.8 %copy-start.74 = (s32[4096]{0:T(1024)S(1)}, s32[4096]{0:T(1024)}, u32[]{:S(2)}) copy-start(s32[4096]{0:T(1024)} %param.29) | copy-start | bytes 49156
  7.2 20.8 %copy-start.75 = (f32[3,256]{1,0:T(4,128)S(1)}, f32[3,256]{1,0:T(4,128)}, u32[]{:S(2)}) copy-start(f32[3,256]{1,0:T(4,128)} %param.39) | copy-start | bytes 9220
  7.2 606.7 %all-reduce.7.cloned.1.call-start = ((), (), s32[]{:S(2)}) async-start(), calls=%async_computation | async-start | bytes 802816 | tf_op jit(solution)/shard_map/psum | solution.py:121
  7.4 16.6 %copy-start.80 = (f32[2,3]{1,0:T(2,128)}, f32[2,3]{1,0:T(2,128)S(1)}, u32[]{:S(2)}) copy-start(f32[2,3]{1,0:T(2,128)S(1)} %broadcast_multiply_fusion.6) | copy-start | bytes 76
  9.6 6.4 %collective-permute-start = (f32[1,64,131]{2,1,0:T(8,128)S(1)}, f32[1,64,131]{2,1,0:T(8,128)S(1)}, u32[]{:S(2)}, u32[]{:S(2)}) collective-permute-start(f32[1,64,131]{2,1,0:T(8,128)S(1)} %get-tuple-element.1573), channel_id=1, source_target_pairs={{0,32},{32,64},{64,96},{96,128},{128,160},{160,192},{192,224},{224... | collective-permute-start | bytes 100616 | tf_op jit(solution)/shard_map/ppermute | solution.py:22
  12.3 3.8 collective-permute-start.1
  13.8 22.0 %copy-start.32 = (f32[4,128]{1,0:T(4,128)S(1)}, f32[4,128]{1,0:T(4,128)}, u32[]{:S(2)}) copy-start(f32[4,128]{1,0:T(4,128)} %param.35) | copy-start | bytes 6148
  13.8 22.0 %copy-start.84 = (s32[256]{0:T(256)S(1)}, s32[256]{0:T(256)}, u32[]{:S(2)}) copy-start(s32[256]{0:T(256)} %param.28) | copy-start | bytes 3076
  16.0 19.8 %copy-start.78 = (f32[2,3]{1,0:T(2,128)}, f32[2,3]{1,0:T(2,128)S(1)}, u32[]{:S(2)}) copy-start(f32[2,3]{1,0:T(2,128)S(1)} %broadcast_multiply_fusion.4) | copy-start | bytes 76
  16.0 86.3 %copy-start.66 = (f32[256]{0:T(256)}, f32[256]{0:T(256)S(1)}, u32[]{:S(2)}) copy-start(f32[256]{0:T(256)S(1)} %fusion.213) | copy-start | bytes 3076
  18.4 5.5 collective-permute-start.2
  19.6 4.4 collective-permute-start.3
  24.9 7.6 %collective-permute-start.4 = (f32[1,64,131]{2,1,0:T(8,128)S(1)}, f32[1,64,131]{2,1,0:T(8,128)S(1)}, u32[]{:S(2)}, u32[]{:S(2)}) collective-permute-start(f32[1,64,131]{2,1,0:T(8,128)S(1)} %get-tuple-element.1567), channel_id=1, source_target_pairs={{0,1},{1,2},{2,3},{3,0},{4,5},{5,6},{6,7},{7,4},{8,9},{9,10},{10,1... | collective-permute-start | bytes 100616 | tf_op jit(solution)/shard_map/ppermute | solution.py:22
  28.0 72.4 %copy-start.76 = (f32[256]{0:T(256)}, f32[256]{0:T(256)S(1)}, u32[]{:S(2)}) copy-start(f32[256]{0:T(256)S(1)} %fusion.212) | copy-start | bytes 3076
  28.2 72.1 %copy-start.21 = (f32[3,256]{0,1:T(8,128)}, f32[3,256]{0,1:T(8,128)S(1)}, u32[]{:S(2)}) copy-start(f32[3,256]{0,1:T(8,128)S(1)} %copy.179) | copy-start | bytes 9220
  28.2 7.0 %collective-permute-start.5 = (f32[1,64,131]{2,1,0:T(8,128)S(1)}, f32[1,64,131]{2,1,0:T(8,128)S(1)}, u32[]{:S(2)}, u32[]{:S(2)}) collective-permute-start(f32[1,64,131]{2,1,0:T(8,128)S(1)} %get-tuple-element.1566), channel_id=1, source_target_pairs={{1,0},{2,1},{3,2},{0,3},{5,4},{6,5},{7,6},{4,7},{9,8},{10,9},{11,1... | collective-permute-start | bytes 100616 | tf_op jit(solution)/shard_map/ppermute | solution.py:23
  65.7 34.6 %copy-start.18 = (f32[256,128]{1,0:T(8,128)S(1)}, f32[256,128]{1,0:T(8,128)}, u32[]{:S(2)}) copy-start(f32[256,128]{1,0:T(8,128)} %param.25) | copy-start | bytes 393220
  65.7 34.6 %copy-start.69 = (f32[3,128]{1,0:T(4,128)S(1)}, f32[3,128]{1,0:T(4,128)}, u32[]{:S(2)}) copy-start(f32[3,128]{1,0:T(4,128)} %param.37) | copy-start | bytes 4612
  65.7 36.8 %copy-start.63 = (s32[2,64]{1,0:T(2,128)S(1)}, s32[2,64]{1,0:T(2,128)}, u32[]{:S(2)}) copy-start(s32[2,64]{1,0:T(2,128)} %param.30) | copy-start | bytes 1540
  65.7 37.1 %copy-start.81 = (f32[2,3]{1,0:T(2,128)S(1)}, f32[2,3]{1,0:T(2,128)}, u32[]{:S(2)}) copy-start(f32[2,3]{1,0:T(2,128)} %copy-done.80) | copy-start | bytes 76
  99.7 16.9 %copy-start.79 = (f32[2,3]{1,0:T(2,128)S(1)}, f32[2,3]{1,0:T(2,128)}, u32[]{:S(2)}) copy-start(f32[2,3]{1,0:T(2,128)} %copy-done.78) | copy-start | bytes 76
  100.3 21.1 %copy-start.39 = (f32[128,128]{1,0:T(8,128)S(1)}, f32[128,128]{1,0:T(8,128)}, u32[]{:S(2)}) copy-start(f32[128,128]{1,0:T(8,128)} %param.34) | copy-start | bytes 196612
  102.3 24.9 %copy-start.16 = (f32[256,128]{1,0:T(8,128)}, f32[256,128]{1,0:T(8,128)S(1)}, u32[]{:S(2)}) copy-start(f32[256,128]{1,0:T(8,128)S(1)} %get-tuple-element.1545) | copy-start | bytes 393220
  103.1 4.9 collective-permute-start.6
  106.6 3.7 collective-permute-start.7
  111.0 5.3 collective-permute-start.8
  111.6 4.8 collective-permute-start.9
  117.3 5.7 collective-permute-start.10
  121.7 4.9 collective-permute-start.11
  187.7 11.9 %copy-start.14 = (f32[128,128]{1,0:T(8,128)S(1)}, f32[128,128]{1,0:T(8,128)}, u32[]{:S(2)}) copy-start(f32[128,128]{1,0:T(8,128)} %get-tuple-element.2119) | copy-start | bytes 196612 | tf_op jit(solution)/shard_map/transpose(jvp())/while
  187.7 11.9 %copy-start.33 = (f32[2,128,128]{2,1,0:T(8,128)S(1)}, f32[2,128,128]{2,1,0:T(8,128)}, u32[]{:S(2)}) copy-start(f32[2,128,128]{2,1,0:T(8,128)} %get-tuple-element.2316) | copy-start | bytes 393220 | tf_op jit(solution)/shard_map/transpose(jvp())/while
  187.7 13.1 %copy-start.41 = (f32[2048]{0:T(1024)S(1)}, f32[2048]{0:T(1024)}, u32[]{:S(2)}) copy-start(f32[2048]{0:T(1024)} %get-tuple-element.2118) | copy-start | bytes 24580 | tf_op jit(solution)/shard_map/transpose(jvp())/while
  220.6 11.9 %copy-start.14 = (f32[128,128]{1,0:T(8,128)S(1)}, f32[128,128]{1,0:T(8,128)}, u32[]{:S(2)}) copy-start(f32[128,128]{1,0:T(8,128)} %get-tuple-element.2119) | copy-start | bytes 196612 | tf_op jit(solution)/shard_map/transpose(jvp())/while
  220.6 11.9 %copy-start.33 = (f32[2,128,128]{2,1,0:T(8,128)S(1)}, f32[2,128,128]{2,1,0:T(8,128)}, u32[]{:S(2)}) copy-start(f32[2,128,128]{2,1,0:T(8,128)} %get-tuple-element.2316) | copy-start | bytes 393220 | tf_op jit(solution)/shard_map/transpose(jvp())/while
  220.6 13.1 %copy-start.41 = (f32[2048]{0:T(1024)S(1)}, f32[2048]{0:T(1024)}, u32[]{:S(2)}) copy-start(f32[2048]{0:T(1024)} %get-tuple-element.2118) | copy-start | bytes 24580 | tf_op jit(solution)/shard_map/transpose(jvp())/while
  245.4 14.6 %copy-start.72 = (s32[2,64]{1,0:T(2,128)S(1)}, s32[2,64]{1,0:T(2,128)}, u32[]{:S(2)}) copy-start(s32[2,64]{1,0:T(2,128)} %param.31) | copy-start | bytes 1540
  245.5 5.4 collective-permute-start.12
  247.8 18.6 %copy-start.20 = (f32[128,128]{1,0:T(8,128)S(1)}, f32[128,128]{1,0:T(8,128)}, u32[]{:S(2)}) copy-start(f32[128,128]{1,0:T(8,128)} %get-tuple-element.1024) | copy-start | bytes 196612
  247.8 4.7 collective-permute-start.13
  252.6 19.0 %copy-start.64 = (s32[2,64]{1,0:T(2,128)S(1)}, s32[2,64]{1,0:T(2,128)}, u32[]{:S(2)}) copy-start(s32[2,64]{1,0:T(2,128)} %param.30) | copy-start | bytes 1540
  253.1 18.9 %copy-start.67 = (f32[256]{0:T(256)S(1)}, f32[256]{0:T(256)}, u32[]{:S(2)}) copy-start(f32[256]{0:T(256)} %copy-done.66) | copy-start | bytes 3076
  253.1 18.9 %copy-start.70 = (f32[3,128]{1,0:T(4,128)S(1)}, f32[3,128]{1,0:T(4,128)}, u32[]{:S(2)}) copy-start(f32[3,128]{1,0:T(4,128)} %param.37) | copy-start | bytes 4612
  253.1 19.2 %copy-start.51 = (f32[2,128,128]{2,1,0:T(8,128)S(1)}, f32[2,128,128]{2,1,0:T(8,128)}, u32[]{:S(2)}) copy-start(f32[2,128,128]{2,1,0:T(8,128)} %copy-done.50) | copy-start | bytes 393220
  253.1 19.2 %copy-start.77 = (f32[256]{0:T(256)S(1)}, f32[256]{0:T(256)}, u32[]{:S(2)}) copy-start(f32[256]{0:T(256)} %copy-done.76) | copy-start | bytes 3076
  253.6 5.3 collective-permute-start.14
  255.1 4.9 collective-permute-start.15
  260.8 7.3 %collective-permute-start.16 = (f32[1,64,131]{2,1,0:T(8,128)S(1)}, f32[1,64,131]{2,1,0:T(8,128)S(1)}, u32[]{:S(2)}, u32[]{:S(2)}) collective-permute-start(f32[1,64,131]{2,1,0:T(8,128)S(1)} %get-tuple-element.1553), channel_id=1, source_target_pairs={{0,32},{32,64},{64,96},{96,128},{128,160},{160,192},{192,224},{224... | collective-permute-start | bytes 100616 | tf_op jit(solution)/shard_map/ppermute | solution.py:22
  267.9 3.7 collective-permute-start.17
  290.3 11.0 %copy-start.15 = (f32[128,128]{1,0:T(8,128)S(1)}, f32[128,128]{1,0:T(8,128)}, u32[]{:S(2)}) copy-start(f32[128,128]{1,0:T(8,128)} %get-tuple-element.2141) | copy-start | bytes 196612 | tf_op jit(solution)/shard_map/transpose(jvp())/while
  290.3 11.0 %copy-start.36 = (f32[2,128,128]{2,1,0:T(8,128)S(1)}, f32[2,128,128]{2,1,0:T(8,128)}, u32[]{:S(2)}) copy-start(f32[2,128,128]{2,1,0:T(8,128)} %get-tuple-element.2382) | copy-start | bytes 393220 | tf_op jit(solution)/shard_map/transpose(jvp())/while
  290.3 11.7 %copy-start.42 = (f32[2048]{0:T(1024)S(1)}, f32[2048]{0:T(1024)}, u32[]{:S(2)}) copy-start(f32[2048]{0:T(1024)} %get-tuple-element.2140) | copy-start | bytes 24580 | tf_op jit(solution)/shard_map/transpose(jvp())/while
  321.3 11.0 %copy-start.36 = (f32[2,128,128]{2,1,0:T(8,128)S(1)}, f32[2,128,128]{2,1,0:T(8,128)}, u32[]{:S(2)}) copy-start(f32[2,128,128]{2,1,0:T(8,128)} %get-tuple-element.2382) | copy-start | bytes 393220 | tf_op jit(solution)/shard_map/transpose(jvp())/while
  321.4 11.7 %copy-start.42 = (f32[2048]{0:T(1024)S(1)}, f32[2048]{0:T(1024)}, u32[]{:S(2)}) copy-start(f32[2048]{0:T(1024)} %get-tuple-element.2140) | copy-start | bytes 24580 | tf_op jit(solution)/shard_map/transpose(jvp())/while
  344.7 13.4 %copy-start.73 = (s32[2,64]{1,0:T(2,128)S(1)}, s32[2,64]{1,0:T(2,128)}, u32[]{:S(2)}) copy-start(s32[2,64]{1,0:T(2,128)} %param.31) | copy-start | bytes 1540
  344.8 6.1 collective-permute-start.18
  346.4 4.7 collective-permute-start.19
  351.6 16.3 %copy-start.65 = (s32[2,64]{1,0:T(2,128)S(1)}, s32[2,64]{1,0:T(2,128)}, u32[]{:S(2)}) copy-start(s32[2,64]{1,0:T(2,128)} %param.30) | copy-start | bytes 1540
  352.1 5.7 collective-permute-start.20
  354.1 3.9 collective-permute-start.21
  359.0 5.2 collective-permute-start.22
  364.2 3.7 collective-permute-start.23
  (78 other events, 368.8 us)
Sparse Core Ops, SparseCore 0:
  364.3 249.5 all-reduce.6
where the time goes:
time: 631 us; the launch traced here: 625 us
  waiting for transfers between devices  273 us (43%)
  matrix products  190 us (30%)
  local copies, waits for them, and re-layouts  66.5 us (11%)
  starting transfers between devices  49.3 us (8%)
  other arithmetic  26.4 us (4%)
  between operations  16.4 us (3%)
    psum x1, waiting for transfers between devices, reduce_grads(): return unpack_grads(lax.psum(pack_grads(grads), ('gx', 'gy', 'gz')), grads)  244 us
    dot_general x36, matrix products, matmul(): jnp.dot(left, right, precision=PRECISE, preferred_element_type=jnp.float32)  116 us
    dot_general x10, matrix products, one_block(): lax.dot_general(table_p, picker, (((1,), (1,)), ((), ())), precision=PREC...  39.2 us
    ppermute x12, starting transfers between devices, padded(): before = lax.ppermute(last, axis, up)  28 us
    another operation x23, local copies, waits for them, and re-layouts  24.1 us
    ppermute x12, starting transfers between devices, padded(): after = lax.ppermute(leading, axis, down)  21.2 us
    dot_general x14, matrix products, one_block(): lax.dot_general(geo, w_geo, (((0,), (0,)), ((), ())), precision=PRECISE,...  18.9 us
    ppermute x12, waiting for transfers between devices, padded(): after = lax.ppermute(leading, axis, down)  18.6 us
  transfers between devices with their start and end apart: 25, of which 19 were waited for; matrix products, arithmetic and copies ran while one was open for 2% of the time, Pallas kernels for 0%

commit v1 on v0

v1 whole, which is shorter than its diff:
```python
import functools
import math

import jax
import jax.numpy as jnp
from jax import lax
from jax.experimental import pallas as pl
from jax.experimental.pallas import tpu as pltpu
from jax.sharding import PartitionSpec as P

MESH = pl.DeviceIdType.MESH
AXES = ("gx", "gy", "gz")
F32 = jnp.float32
BF16 = jnp.bfloat16
STRIDE = 0.1
LAT = 128
OWN = 256
NBR = 16
SIDE = 64
GHOST = 2 * SIDE
ROWS = OWN + 3 * GHOST
GRAD_ROWS = 512
MSG = SIDE + 8
UNROLL = 2


def dot(left, right):
    return lax.dot_general(left, right, (((1,), (0,)), ((), ())), preferred_element_type=F32)


def dot_nt(left, right):
    return lax.dot_general(left, right, (((1,), (1,)), ((), ())), preferred_element_type=F32)


def split(value):
    high = value.astype(BF16)
    return high, (value - high.astype(F32)).astype(BF16)


def exact(product, left, right):
    left_high, left_low = split(left)
    right_high, right_low = split(right)
    return product(left_high, right_high) + (product(left_low, right_high) + product(left_high, right_low))


def split_rows(field_x, field_q):
    high, low = split(field_x)
    first = field_q.astype(BF16).astype(F32)
    rest = field_q - first
    second = rest.astype(BF16).astype(F32)
    third = rest - second
    upper = jnp.concatenate([first, second], axis=0).astype(BF16)
    lower = jnp.concatenate([third, jnp.zeros_like(third)], axis=0).astype(BF16)
    return high, low, upper, lower


def join_rows(product):
    value = product[0:LAT] + product[LAT : 2 * LAT]
    base = 2 * LAT
    place = product[base : base + 8] + product[base + 8 : base + 16] + product[base + 16 : base + 24]
    return value, place


def kernel(
    sizes,
    scale,
    latent_ref,
    position_ref,
    senders_ref,
    count_ref,
    ghost_ref,
    particles_ref,
    w_send_ref,
    w_recv_ref,
    w_geo_ref,
    w_msg_ref,
    w_dec_ref,
    cot_latent_ref,
    cot_position_ref,
    out_latent_ref,
    out_position_ref,
    out_send_ref,
    out_recv_ref,
    out_geo_ref,
    out_msg_ref,
    out_dec_ref,
    onehot,
    sel_x,
    sel_y,
    sel_z,
    tab_x,
    tab_q,
    tab_s,
    tab_a,
    gath,
    slope,
    geos,
    summed,
    fresh,
    dpre,
    d_recv,
    d_place,
    cot_x,
    cot_q,
    pad,
    w_t,
    w_geo_k,
    w_geo_s,
    d_geo,
    grads,
    part_x,
    part_y,
    part_z,
    got_x,
    got_y,
    total,
    send_buf,
    recv_buf,
    halo_send,
    halo_recv,
    sum_send,
    sum_recv,
):
    index = tuple(lax.axis_index(axis) for axis in AXES)
    sels = (sel_x, sel_y, sel_z)

    barrier = pltpu.get_barrier_semaphore()
    partners = 0
    for axis in range(3):
        for k in range(1, sizes[axis]):
            peer = lax.rem(index[axis] + k, sizes[axis])
            pl.semaphore_signal(barrier, inc=1, device_id={AXES[axis]: peer}, device_id_type=MESH)
            partners += 1

    lane = lax.broadcasted_iota(jnp.int32, (SIDE, GHOST), 1)
    left = lane < SIDE
    left8 = left[0:8]
    row8 = lax.broadcasted_iota(jnp.int32, (8, GHOST), 0)
    row8_own = lax.broadcasted_iota(jnp.int32, (8, OWN), 0)
    live = (lax.broadcasted_iota(jnp.int32, (1, OWN), 1) < particles_ref[0]).astype(F32)

    pending = []

    def start_halo(phase, axis, field_x, field_q):
        turned = pltpu.roll(field_x, SIDE, 1)
        turned_q = pltpu.roll(field_q, SIDE, 1)
        send_buf[phase, 0, 0:SIDE, :] = jnp.where(left, field_x[0:SIDE], turned[SIDE:])
        send_buf[phase, 0, SIDE:MSG, :] = turned_q
        send_buf[phase, 1, 0:SIDE, :] = jnp.where(left, turned[0:SIDE], field_x[SIDE:])
        send_buf[phase, 1, SIDE:MSG, :] = turned_q
        size = sizes[axis]
        lower = lax.rem(index[axis] + size - 1, size)
        upper = lax.rem(index[axis] + 1, size)
        copies = []
        for side, peer in ((0, lower), (1, upper)):
            copy = pltpu.make_async_remote_copy(
                src_ref=send_buf.at[phase, side],
                dst_ref=recv_buf.at[phase, 1 - side],
                send_sem=halo_send.at[phase, side],
                recv_sem=halo_recv.at[phase, 1 - side],
                device_id={AXES[axis]: peer},
                device_id_type=MESH,
            )
            copy.start()
            copies.append(copy)
        pending.extend(copies)
        return copies

    def end_halo(phase, copies):
        for copy in copies:
            copy.wait_recv()
        before = recv_buf[phase, 0, 0:SIDE, :]
        after = recv_buf[phase, 1, 0:SIDE, :]
        top = jnp.where(left, before, pltpu.roll(after, SIDE, 1))
        bottom = jnp.where(left, pltpu.roll(before, SIDE, 1), after)
        field_q = jnp.where(left8, recv_buf[phase, 0, SIDE:MSG, :], recv_buf[phase, 1, SIDE:MSG, :])
        return jnp.concatenate([top, bottom], axis=0), field_q

    def set_block(step, start, width, field_x, field_q):
        cols = slice(start, start + width)
        tab_x[step, :, cols] = field_x
        tab_q[step, :, cols] = field_q
        high, low, upper, lower = split_rows(field_x, field_q)
        tab_s[0:LAT, cols] = high
        tab_s[LAT : 2 * LAT, cols] = low
        tab_s[256:272, cols] = upper
        tab_s[272:288, cols] = lower

    def project_block(step, start, width):
        cols = slice(start, start + width)
        high, low = split(exact(dot, w_t[0], tab_x[step, :, cols]))
        tab_a[0:LAT, cols] = high
        tab_a[LAT : 2 * LAT, cols] = low
        tab_a[256:288, cols] = tab_s[256:288, cols]

    def select(axis, start, width):
        return dot(tab_s[:, start : start + width], sels[axis][start : start + width, :])

    def send_rows(phase, axis, product):
        field_x, field_q = join_rows(product)
        low = jnp.where(index[axis] == 0, float(sizes[axis]), 0.0)
        high = jnp.where(index[axis] == sizes[axis] - 1, -float(sizes[axis]), 0.0)
        offset = jnp.where(row8 == axis, jnp.where(left8, low, high), 0.0)
        return start_halo(phase, axis, field_x, field_q + offset)

    def gather_block(start, width, extra=None):
        def body(n, carry):
            value, place = join_rows(dot(tab_a[:, start : start + width], onehot[n, start : start + width, :]))
            if extra is None:
                gath[n, 0:LAT, :] += value
                gath[n, LAT:, :] += place
            else:
                gath[n, 0:LAT, :] = value + extra[...]
                gath[n, LAT:, :] = place
            return carry

        lax.fori_loop(0, NBR, body, 0, unroll=UNROLL)

    def forward(step, phase, prologue):
        copies = send_rows(phase, 0, select(0, 0, OWN))
        prologue()
        project_block(step, 0, OWN)
        d_recv[...] = exact(dot, w_t[1], tab_x[step, :, 0:OWN])
        early_y = select(1, 0, OWN)
        early_z = select(2, 0, OWN)
        gather_block(0, OWN, d_recv)
        start = OWN
        set_block(step, start, GHOST, *end_halo(phase, copies))
        copies = send_rows(phase + 1, 1, early_y + select(1, start, GHOST))
        early_z = early_z + select(2, start, GHOST)
        project_block(step, start, GHOST)
        gather_block(start, GHOST)
        start = start + GHOST
        set_block(step, start, GHOST, *end_halo(phase + 1, copies))
        copies = send_rows(phase + 2, 2, early_z + select(2, start, GHOST))
        project_block(step, start, GHOST)
        gather_block(start, GHOST)
        start = start + GHOST
        set_block(step, start, GHOST, *end_halo(phase + 2, copies))
        project_block(step, start, GHOST)
        own_q = tab_q[step, :, 0:OWN]
        counts = count_ref[...]
        summed[step] = jnp.zeros((LAT, OWN), F32)

        def body(n, carry):
            value, place = join_rows(dot(tab_a[:, start : start + GHOST], onehot[n, start : start + GHOST, :]))
            rel = gath[n, LAT:, :] + place - own_q
            dist = jnp.sum(rel * rel, axis=0, keepdims=True)
            geo = jnp.where(row8_own == 3, dist, rel)
            geos[step, n] = geo
            coarse = geo.astype(BF16).astype(F32)
            fine = geo - coarse
            rows = jnp.concatenate([coarse, fine, coarse, jnp.zeros_like(fine)], axis=0).astype(BF16)
            pre = gath[n, 0:LAT, :] + value + dot(w_geo_k[...], rows)
            gate = 0.5 * jnp.tanh(0.5 * pre) + 0.5
            keep = (counts > n).astype(F32)
            gate_keep = gate * keep
            summed[step] += pre * gate_keep
            slope[step, n] = gate_keep * (1.0 + pre * (1.0 - gate))
            return carry

        lax.fori_loop(0, NBR, body, 0, unroll=UNROLL)
        new_x = tab_x[step, :, 0:OWN] + live * exact(dot, w_t[2], summed[step])
        fresh[step] = new_x
        return new_x

    def scatter(start, width):
        def body(n, carry):
            return carry + dot_nt(dpre[n], onehot[n, start : start + width, :])

        product = lax.fori_loop(0, NBR, body, jnp.zeros((272, width), F32), unroll=UNROLL)
        return product[0:LAT] + product[LAT : 2 * LAT], product[256:264] + product[264:272]

    def backward(step, phase, cot_v, cot_p, first, tail):
        move = STRIDE * live * cot_p
        full = cot_v
        for k in range(3):
            full = full + w_t[3, :, k : k + 1] * move[k : k + 1, :]
        d_agg = live * full
        d_sum = exact(dot, w_msg_ref[...], d_agg)
        d_recv[...] = jnp.zeros((LAT, OWN), F32)
        d_place[...] = jnp.zeros((8, OWN), F32)
        d_geo[...] = jnp.zeros((8, LAT), F32)

        def body(n, carry):
            value = d_sum * slope[step, n]
            geo = geos[step, n]
            high, low = split(value)
            dpre[n, 0:LAT, :] = high
            dpre[n, LAT : 2 * LAT, :] = low
            d_recv[...] += value
            main = dot(w_geo_s[...], high)
            side = dot(w_geo_s[...], low)
            back = main[0:8] + main[8:16] + side[0:8]
            d_rel = jnp.where(row8_own < 3, back + 2.0 * geo * back[3:4], 0.0)
            d_place[...] -= d_rel
            coarse = d_rel.astype(BF16).astype(F32)
            dpre[n, 256:272, :] = jnp.concatenate([coarse, d_rel - coarse], axis=0).astype(BF16)
            geo_high = geo.astype(BF16).astype(F32)
            geo_rows = jnp.concatenate([geo_high, geo - geo_high], axis=0).astype(BF16)
            main = dot_nt(geo_rows, high)
            side = dot_nt(geo_rows, low)
            d_geo[...] += main[0:8] + main[8:16] + side[0:8]
            return carry

        lax.fori_loop(0, NBR, body, 0, unroll=UNROLL)

        start = OWN + 2 * GHOST
        d_send, d_q = scatter(start, GHOST)
        copies = start_halo(phase, 2, exact(dot, w_send_ref[...], d_send), d_q)
        d_weight = exact(dot_nt, tab_x[step, :, start : start + GHOST], d_send)
        for start, width in ((OWN + GHOST, GHOST), (OWN, GHOST), (0, OWN)):
            d_send, d_q = scatter(start, width)
            cot_x[:, start : start + width] = exact(dot, w_send_ref[...], d_send)
            cot_q[:, start : start + width] = d_q
            d_weight = d_weight + exact(dot_nt, tab_x[step, :, start : start + width], d_send)
        cot_x[:, 0:OWN] += full + exact(dot, w_recv_ref[...], d_recv[...])
        cot_q[:, 0:OWN] += cot_p + d_place[...]
        pieces = (
            (0, LAT, d_weight),
            (LAT, LAT, exact(dot_nt, tab_x[step, :, 0:OWN], d_recv[...])),
            (2 * LAT, LAT, exact(dot_nt, summed[step], d_agg)),
            (3 * LAT, 8, d_geo[...]),
            (3 * LAT + 8, 8, exact(dot_nt, move, fresh[step])),
        )
        for base, rows, piece in pieces:
            if first:
                grads[base : base + rows, :] = piece
            else:
                grads[base : base + rows, :] += piece
        tail(0)

        def arrived(number, axis, copies):
            field_x, field_q = end_halo(number, copies)
            high, low = split(field_x)
            coarse = field_q.astype(BF16).astype(F32)
            rows = jnp.concatenate([coarse, field_q - coarse], axis=0).astype(BF16)

            def add(start, width):
                sel = sels[axis][start : start + width, :]
                extra = dot_nt(high, sel) + dot_nt(low, sel)
                extra_q = dot_nt(rows, sel)
                cot_x[:, start : start + width] += extra
                cot_q[:, start : start + width] += extra_q[0:8] + extra_q[8:16]

            return add

        add = arrived(phase, 2, copies)
        start = OWN + GHOST
        add(start, GHOST)
        copies = start_halo(phase + 1, 1, cot_x[:, start : start + GHOST], cot_q[:, start : start + GHOST])
        add(OWN, GHOST)
        add(0, OWN)
        add = arrived(phase + 1, 1, copies)
        start = OWN
        add(start, GHOST)
        copies = start_halo(phase + 2, 0, cot_x[:, start : start + GHOST], cot_q[:, start : start + GHOST])
        add(0, OWN)
        tail(1)
        add = arrived(phase + 2, 0, copies)
        add(0, OWN)
        return cot_x[:, 0:OWN], cot_q[:, 0:OWN]

    pad[...] = jnp.zeros((8, OWN), F32)
    pad[0:3, :] = position_ref[...]
    set_block(0, 0, OWN, jnp.transpose(latent_ref[...]), pad[...])
    sel_x[...] = (lax.broadcasted_iota(jnp.int32, (OWN, GHOST), 0) == ghost_ref[0:1, :]).astype(F32).astype(BF16)
    pl.semaphore_wait(barrier, partners)

    def prologue():
        for axis in (1, 2):
            rows = OWN + axis * GHOST
            ids = lax.broadcasted_iota(jnp.int32, (rows, GHOST), 0)
            sels[axis][...] = (ids == ghost_ref[axis : axis + 1, :]).astype(F32).astype(BF16)
        w_t[0] = jnp.transpose(w_send_ref[...])
        w_t[1] = jnp.transpose(w_recv_ref[...])
        w_t[2] = jnp.transpose(w_msg_ref[...])
        w_t[3] = jnp.zeros((LAT, LAT), F32)
        w_t[3, 0:3, :] = w_dec_ref[...]
        w_t[3] = jnp.transpose(w_t[3])
        w_t[4] = jnp.zeros((LAT, LAT), F32)
        w_t[4, 0:4, :] = w_geo_ref[...]
        w_geo = w_t[4, 0:8, :]
        coarse = w_geo.astype(BF16).astype(F32)
        fine = w_geo - coarse
        w_geo_s[...] = jnp.concatenate([coarse, fine], axis=0).astype(BF16)
        w_t[4, 0:8, :] = coarse
        w_t[4, 8:16, :] = coarse
        w_t[4, 16:24, :] = fine
        w_geo_k[...] = jnp.transpose(w_t[4])[:, 0:32].astype(BF16)
        grads[...] = jnp.zeros((GRAD_ROWS, LAT), F32)

        def body(n, carry):
            ids = lax.broadcasted_iota(jnp.int32, (ROWS, OWN), 0)
            onehot[n] = (ids == senders_ref[pl.ds(n, 1), :]).astype(F32).astype(BF16)
            return carry

        lax.fori_loop(0, NBR, body, 0)

    new_x = forward(0, 0, prologue)
    w_dec = jnp.concatenate([w_dec_ref[...], jnp.zeros((5, LAT), F32)], axis=0)
    new_q = tab_q[0, :, 0:OWN] + STRIDE * live * exact(dot, w_dec, new_x)
    set_block(1, 0, OWN, new_x, new_q)
    forward(1, 3, lambda: None)

    pad[0:3, :] = cot_position_ref[...]
    cot_v, cot_p = backward(1, 6, jnp.transpose(cot_latent_ref[...]), pad[...], True, lambda number: None)

    piece_x = GRAD_ROWS // sizes[0]
    piece_y = piece_x // sizes[1]
    bases = (0, sizes[0] - 1, sizes[0] + sizes[1] - 2)
    more = bases[2] + sizes[2] - 1

    def exchange(axis, base, source, target):
        copies = []
        for k in range(1, sizes[axis]):
            peer = lax.rem(index[axis] + k, sizes[axis])
            copy = pltpu.make_async_remote_copy(
                src_ref=source(peer),
                dst_ref=target(k),
                send_sem=sum_send.at[base + k - 1],
                recv_sem=sum_recv.at[base + k - 1],
                device_id={AXES[axis]: peer},
                device_id_type=MESH,
            )
            copy.start()
            copies.append(copy)
        pending.extend(copies)
        return copies

    state = {}

    def tail(number):
        if number == 0:
            state["x"] = exchange(
                0,
                bases[0],
                lambda peer: grads.at[pl.ds(pl.multiple_of(peer * piece_x, 8), piece_x), :],
                lambda k: got_x.at[k - 1],
            )
        else:
            for copy in state["x"]:
                copy.wait_recv()
            value = grads[pl.ds(pl.multiple_of(index[0] * piece_x, 8), piece_x), :]
            for k in range(sizes[0] - 1):
                value = value + got_x[k]
            part_x[...] = value
            state["y"] = exchange(
                1,
                bases[1],
                lambda peer: part_x.at[pl.ds(pl.multiple_of(peer * piece_y, 8), piece_y), :],
                lambda k: got_y.at[k - 1],
            )

    cot_v, cot_p = backward(0, 9, cot_v, cot_p, False, tail)
    for copy in state["y"]:
        copy.wait_recv()
    value = part_x[pl.ds(pl.multiple_of(index[1] * piece_y, 8), piece_y), :]
    for k in range(sizes[1] - 1):
        value = value + got_y[k]
    part_z[index[2]] = value
    copies = exchange(2, bases[2], lambda peer: part_z.at[index[2]], lambda k: part_z.at[index[2]])
    out_latent_ref[...] = jnp.transpose(cot_v)
    out_position_ref[...] = cot_p[0:3]
    for copy in copies:
        copy.wait_recv()
    value = part_z[0]
    for k in range(1, sizes[2]):
        value = value + part_z[k]
    own_y = pl.ds(pl.multiple_of(index[1] * piece_y, 8), piece_y)
    part_y[own_y, :] = value * scale
    copies = exchange(1, more, lambda peer: part_y.at[own_y, :], lambda k: part_y.at[own_y, :])
    for copy in copies:
        copy.wait_recv()
    own_x = pl.ds(pl.multiple_of(index[0] * piece_x, 8), piece_x)
    total[own_x, :] = part_y[...]
    copies = exchange(0, more + sizes[1] - 1, lambda peer: part_y, lambda k: total.at[own_x, :])
    for copy in copies:
        copy.wait_recv()
    out_send_ref[...] = total[0:LAT, :]
    out_recv_ref[...] = total[LAT : 2 * LAT, :]
    out_msg_ref[...] = total[2 * LAT : 3 * LAT, :]
    out_geo_ref[...] = total[3 * LAT : 3 * LAT + 4, :]
    out_dec_ref[...] = total[3 * LAT + 8 : 3 * LAT + 11, :]
    for copy in pending:
        copy.wait_send()


def per_device(sizes, scale, *args):
    (
        latent,
        position,
        particle_count,
        nbr_count,
        senders,
        ghost_x,
        ghost_y,
        ghost_z,
        w_send,
        w_recv,
        w_geo,
        w_msg,
        w_dec,
        cot_latent,
        cot_position,
    ) = args
    slots = jnp.transpose(senders.reshape(OWN, NBR))
    counts = nbr_count.reshape(1, OWN)
    ghosts = jnp.stack([ghost_x.reshape(-1), ghost_y.reshape(-1), ghost_z.reshape(-1)])
    nx, ny, nz = sizes
    piece_x = GRAD_ROWS // nx
    piece_y = piece_x // ny
    sums = 2 * (nx - 1) + 2 * (ny - 1) + (nz - 1)
    vmem = pl.BlockSpec(memory_space=pltpu.VMEM)
    smem = pl.BlockSpec(memory_space=pltpu.SMEM)
    return pl.pallas_call(
        functools.partial(kernel, sizes, scale),
        out_shape=(
            jax.ShapeDtypeStruct((OWN, LAT), F32),
            jax.ShapeDtypeStruct((3, OWN), F32),
            jax.ShapeDtypeStruct((LAT, LAT), F32),
            jax.ShapeDtypeStruct((LAT, LAT), F32),
            jax.ShapeDtypeStruct((4, LAT), F32),
            jax.ShapeDtypeStruct((LAT, LAT), F32),
            jax.ShapeDtypeStruct((3, LAT), F32),
        ),
        in_specs=[vmem] * 5 + [smem] + [vmem] * 7,
        out_specs=(vmem,) * 7,
        scratch_shapes=[
            pltpu.VMEM((NBR, ROWS, OWN), BF16),
            pltpu.VMEM((OWN, GHOST), BF16),
            pltpu.VMEM((OWN + GHOST, GHOST), BF16),
            pltpu.VMEM((OWN + 2 * GHOST, GHOST), BF16),
            pltpu.VMEM((2, LAT, ROWS), F32),
            pltpu.VMEM((2, 8, ROWS), F32),
            pltpu.VMEM((288, ROWS), BF16),
            pltpu.VMEM((288, ROWS), BF16),
            pltpu.VMEM((NBR, LAT + 8, OWN), F32),
            pltpu.VMEM((2, NBR, LAT, OWN), F32),
            pltpu.VMEM((2, NBR, 8, OWN), F32),
            pltpu.VMEM((2, LAT, OWN), F32),
            pltpu.VMEM((2, LAT, OWN), F32),
            pltpu.VMEM((NBR, 272, OWN), BF16),
            pltpu.VMEM((LAT, OWN), F32),
            pltpu.VMEM((8, OWN), F32),
            pltpu.VMEM((LAT, ROWS), F32),
            pltpu.VMEM((8, ROWS), F32),
            pltpu.VMEM((8, OWN), F32),
            pltpu.VMEM((5, LAT, LAT), F32),
            pltpu.VMEM((LAT, 32), BF16),
            pltpu.VMEM((16, LAT), BF16),
            pltpu.VMEM((8, LAT), F32),
            pltpu.VMEM((GRAD_ROWS, LAT), F32),
            pltpu.VMEM((piece_x, LAT), F32),
            pltpu.VMEM((piece_x, LAT), F32),
            pltpu.VMEM((nz, piece_y, LAT), F32),
            pltpu.VMEM((nx - 1, piece_x, LAT), F32),
            pltpu.VMEM((ny - 1, piece_y, LAT), F32),
            pltpu.VMEM((GRAD_ROWS, LAT), F32),
            pltpu.VMEM((12, 2, MSG, GHOST), F32),
            pltpu.VMEM((12, 2, MSG, GHOST), F32),
            pltpu.SemaphoreType.DMA((12, 2)),
            pltpu.SemaphoreType.DMA((12, 2)),
            pltpu.SemaphoreType.DMA((sums,)),
            pltpu.SemaphoreType.DMA((sums,)),
        ],
        compiler_params=pltpu.CompilerParams(
            collective_id=0, has_side_effects=True, vmem_limit_bytes=48 * 1024 * 1024
        ),
        name="evolver_backward",
    )(
        latent,
        position,
        slots,
        counts,
        ghosts,
        particle_count,
        w_send,
        w_recv,
        w_geo,
        w_msg,
        w_dec,
        cot_latent,
        cot_position,
    )


def solution(mesh):
    sizes = tuple(mesh.shape[axis] for axis in AXES)
    scale = 1.0 / math.sqrt(sizes[0] * sizes[1] * sizes[2] * OWN)
    whole = P(AXES)
    rows = P(AXES, None)
    columns = P(None, AXES)
    placed = (rows, columns, whole, whole, whole, rows, rows, rows) + (P(),) * 5 + (rows, columns)
    return jax.shard_map(
        functools.partial(per_device, sizes, scale),
        mesh=mesh,
        in_specs=placed,
        out_specs=(rows, columns) + (P(),) * 5,
        check_vma=False,
    )
```

time: 631 us -> 107 us (0.17)
  waiting for transfers between devices: 273 us -> 0 us
  matrix products: 190 us -> 0 us
  Pallas kernels: 0 us -> 94.9 us
  local copies, waits for them, and re-layouts: 66.5 us -> 10.5 us
  starting transfers between devices: 49.3 us -> 0 us
  other arithmetic: 26.4 us -> 0.01 us
  between operations: 16.4 us -> 1.37 us
    psum x1 -> x0, waiting for transfers between devices: 244 us -> none  [reduce_grads(): return unpack_grads(lax.psum(pack_grads(grads), ('gx', 'gy', 'gz')), grads)]
    dot_general x89 -> x0, matrix products: 190 us -> none  [the longest x36 116 us: matmul(): jnp.dot(left, right, precision=PRECISE, preferred_element_type=jnp.float32)]
    pallas_call x0 -> x1, Pallas kernels: none -> 94.9 us  [per_device(): pl.pallas_call(functools.partial(kernel, sizes, scale), out_shape=(jax.Sh...]
    ppermute x24 -> x0, starting transfers between devices: 49.2 us -> none  [the longest x12 28 us: padded(): before = lax.ppermute(last, axis, up)]
    ppermute x24 -> x0, waiting for transfers between devices: 29.4 us -> none  [the longest x12 18.6 us: padded(): after = lax.ppermute(leading, axis, down)]
    another operation x41 -> x3, local copies, waits for them, and re-layouts: 24.3 us -> 0.24 us  [per_device(): jnp.stack([ghost_x.reshape(-1), ghost_y.reshape(-1), ghost_z.reshape(-1)])]
    while x126 -> x0, local copies, waits for them, and re-layouts: 12.6 us -> none
    mul x15 -> x0, other arithmetic: 10.4 us -> none  [the longest x8 6.01 us: one_block(): return jnp.sum((message * keep).reshape(BLOCK, slots, -1), axis=1)]
  transfers between devices with their start and end apart: 25 -> 0, of which waited for: 19 -> 0; matrix products, arithmetic and copies ran while one was open for 2% -> 0% of each run, Pallas kernels for 0% -> 0%
where the time goes in v1:
time: 107 us
  Pallas kernels  94.9 us (89%)
  local copies, waits for them, and re-layouts  10.5 us (10%)
  between operations  1.37 us (1%)
    pallas_call x1, Pallas kernels, per_device(): pl.pallas_call(functools.partial(kernel, sizes, scale), out_shape=(jax.Sh...  94.9 us
    unnamed x33, local copies, waits for them, and re-layouts  9.38 us

profile of v1, /device:TPU:1, one launch (start us, length us, event | category | flops | bytes accessed | tf_op | source)
XLA Modules:
  0.0 106.8 jit_solution(7844763216459124806)
XLA Ops:
  1.3 0.0 copy-start.10
  1.3 0.7 copy-done.10
  2.0 0.0 copy-start.11
  2.0 0.1 stack_reshape.9
  2.0 0.6 copy-done.11
  2.6 0.0 copy-start.12
  2.6 0.1 stack_reshape.10
  2.7 0.6 copy-done.12
  3.3 0.1 stack_reshape.11
  3.4 0.0 copy-start
  3.4 0.0 copy-start.1
  3.4 0.9 reshape.20
  4.3 0.0 copy-start.5
  4.3 0.0 copy-start.6
  4.3 0.0 copy-start.7
  4.3 0.0 copy-start.8
  4.3 0.1 copy.22
  4.4 0.0 copy-start.9
  4.4 0.0 copy-done
  4.4 0.0 copy-done.1
  4.4 0.6 copy-done.5
  5.0 0.0 copy-done.6
  5.0 0.0 copy-done.7
  5.0 0.0 copy-done.8
  5.0 0.1 copy-done.9
  5.1 0.0 copy-start.2
  5.1 0.8 copy-done.2
  5.9 0.0 copy-start.3
  5.9 0.8 copy-done.3
  6.8 0.0 copy-start.4
  6.8 0.8 copy-done.4
  7.6 94.9 %evolver_backward.1 = (f32[256,128]{1,0:T(8,128)S(1)}, f32[3,256]{1,0:T(4,128)S(1)}, f32[128,128]{1,0:T(8,128)S(1)}, f32[128,128]{1,0:T(8,128)S(1)}, f32[4,128]{...) custom-call(f32[256,128]{1,0:T(8,128)S(1)} %copy-done, f32[3,256]{1,0:T(4,128)S(1)} %copy-done.5, ...), custom_call_target="tpu_custom_call" | custom-call | tf_op jit(solution)/shard_map/evolver_backward/pallas_call | solution.py:516
  102.5 0.7 copy.31
  103.2 0.6 copy.32
  103.8 0.6 copy.33
  104.4 0.6 copy.34
  105.1 0.6 copy.35
  105.6 0.6 copy.36
  106.3 0.6 copy.37
  (1 shorter events, 0.0 us)
Async XLA Ops:
  1.3 0.7 copy-start.10
  2.0 0.7 copy-start.11
  2.6 0.7 copy-start.12
  3.4 1.0 copy-start
  3.4 1.0 copy-start.1
  4.3 0.7 copy-start.5
  4.3 0.7 copy-start.6
  4.3 0.7 copy-start.7
  4.3 0.7 copy-start.8
  4.4 0.7 copy-start.9
  5.1 0.8 copy-start.2
  5.9 0.8 copy-start.3
  6.8 0.8 copy-start.4

commit v2 on v1

--- a/solution.py
+++ b/solution.py
@@ -21,7 +21,8 @@
 ROWS = OWN + 3 * GHOST
 GRAD_ROWS = 512
 MSG = SIDE + 8
-UNROLL = 2
+UNROLL = 8
+INPUTS = 15
 
 
 def dot(left, right):
@@ -64,26 +65,24 @@
 def kernel(
     sizes,
     scale,
-    latent_ref,
-    position_ref,
-    senders_ref,
-    count_ref,
-    ghost_ref,
-    particles_ref,
-    w_send_ref,
-    w_recv_ref,
-    w_geo_ref,
-    w_msg_ref,
-    w_dec_ref,
-    cot_latent_ref,
-    cot_position_ref,
+    *refs,
+):
+    given = refs[:INPUTS]
+    out_latent_ref, out_position_ref, total = refs[INPUTS : INPUTS + 3]
+    held = refs[INPUTS + 3 : 2 * INPUTS + 3]
+    load_sem = refs[2 * INPUTS + 3]
+    body(sizes, scale, given, held, load_sem, out_latent_ref, out_position_ref, total, *refs[2 * INPUTS + 4 :])
+
+
+def body(
+    sizes,
+    scale,
+    given,
+    held,
+    load_sem,
     out_latent_ref,
     out_position_ref,
-    out_send_ref,
-    out_recv_ref,
-    out_geo_ref,
-    out_msg_ref,
-    out_dec_ref,
+    total,
     onehot,
     sel_x,
     sel_y,
@@ -113,14 +112,38 @@
     part_z,
     got_x,
     got_y,
-    total,
     send_buf,
     recv_buf,
     halo_send,
     halo_recv,
     sum_send,
     sum_recv,
+    slots,
 ):
+    (
+        latent_ref,
+        position_ref,
+        particles_ref,
+        count_ref,
+        senders_ref,
+        ghost_x_ref,
+        ghost_y_ref,
+        ghost_z_ref,
+        w_send_ref,
+        w_recv_ref,
+        w_geo_ref,
+        w_msg_ref,
+        w_dec_ref,
+        cot_latent_ref,
+        cot_position_ref,
+    ) = held
+    ghost_refs = (ghost_x_ref, ghost_y_ref, ghost_z_ref)
+    loads = [
+        pltpu.make_async_copy(source, target, load_sem.at[number])
+        for number, (source, target) in enumerate(zip(given, held))
+    ]
+    for load in loads:
+        load.start()
     index = tuple(lax.axis_index(axis) for axis in AXES)
     sels = (sel_x, sel_y, sel_z)
 
@@ -137,7 +160,16 @@
     left8 = left[0:8]
     row8 = lax.broadcasted_iota(jnp.int32, (8, GHOST), 0)
     row8_own = lax.broadcasted_iota(jnp.int32, (8, OWN), 0)
+    for load in loads:
+        load.wait()
     live = (lax.broadcasted_iota(jnp.int32, (1, OWN), 1) < particles_ref[0]).astype(F32)
+
+    def selector(axis):
+        rows = OWN + axis * GHOST
+        lists = ghost_refs[axis][...]
+        chosen = jnp.concatenate([lists[0:1], lists[1:2]], axis=1)
+        ids = lax.broadcasted_iota(jnp.int32, (rows, GHOST), 0)
+        sels[axis][...] = (ids == chosen).astype(F32).astype(BF16)
 
     pending = []
 
@@ -364,14 +396,12 @@
     pad[...] = jnp.zeros((8, OWN), F32)
     pad[0:3, :] = position_ref[...]
     set_block(0, 0, OWN, jnp.transpose(latent_ref[...]), pad[...])
-    sel_x[...] = (lax.broadcasted_iota(jnp.int32, (OWN, GHOST), 0) == ghost_ref[0:1, :]).astype(F32).astype(BF16)
+    selector(0)
     pl.semaphore_wait(barrier, partners)
 
     def prologue():
-        for axis in (1, 2):
-            rows = OWN + axis * GHOST
-            ids = lax.broadcasted_iota(jnp.int32, (rows, GHOST), 0)
-            sels[axis][...] = (ids == ghost_ref[axis : axis + 1, :]).astype(F32).astype(BF16)
+        selector(1)
+        selector(2)
         w_t[0] = jnp.transpose(w_send_ref[...])
         w_t[1] = jnp.transpose(w_recv_ref[...])
         w_t[2] = jnp.transpose(w_msg_ref[...])
@@ -390,9 +420,21 @@
         w_geo_k[...] = jnp.transpose(w_t[4])[:, 0:32].astype(BF16)
         grads[...] = jnp.zeros((GRAD_ROWS, LAT), F32)
 
+        flat = senders_ref[...]
+        spread = jnp.broadcast_to(flat[:, None, :], (OWN // 8, 8, LAT)).reshape(OWN, LAT)
+        lanes = lax.broadcasted_iota(jnp.int32, (OWN, LAT), 1)
+        sublanes = lax.broadcasted_iota(jnp.int32, (OWN, LAT), 0)
+        mine = lanes // NBR == sublanes % 8
+        rest = spread % 8
+        slot = lax.broadcasted_iota(jnp.int32, (NBR, LAT), 1) % NBR == lax.broadcasted_iota(jnp.int32, (NBR, LAT), 0)
+        slot = slot.astype(F32).astype(BF16)
+        coarse = jnp.where(mine, spread - rest, 0).astype(F32).astype(BF16)
+        fine = jnp.where(mine, rest, 0).astype(F32).astype(BF16)
+        slots[...] = (dot_nt(slot, coarse) + dot_nt(slot, fine)).astype(jnp.int32)
+
         def body(n, carry):
             ids = lax.broadcasted_iota(jnp.int32, (ROWS, OWN), 0)
-            onehot[n] = (ids == senders_ref[pl.ds(n, 1), :]).astype(F32).astype(BF16)
+            onehot[n] = (ids == slots[pl.ds(n, 1), :]).astype(F32).astype(BF16)
             return carry
 
         lax.fori_loop(0, NBR, body, 0)
@@ -477,13 +519,25 @@
     copies = exchange(0, more + sizes[1] - 1, lambda peer: part_y, lambda k: total.at[own_x, :])
     for copy in copies:
         copy.wait_recv()
-    out_send_ref[...] = total[0:LAT, :]
-    out_recv_ref[...] = total[LAT : 2 * LAT, :]
-    out_msg_ref[...] = total[2 * LAT : 3 * LAT, :]
-    out_geo_ref[...] = total[3 * LAT : 3 * LAT + 4, :]
-    out_dec_ref[...] = total[3 * LAT + 8 : 3 * LAT + 11, :]
     for copy in pending:
         copy.wait_send()
+
+
+def hand_out(grad_x, grad_q, total, out_x, out_q, out_send, out_recv, out_geo, out_msg, out_dec, sems):
+    pairs = (
+        (grad_x, out_x),
+        (grad_q, out_q),
+        (total.at[0:LAT, :], out_send),
+        (total.at[LAT : 2 * LAT, :], out_recv),
+        (total.at[3 * LAT : 3 * LAT + 4, :], out_geo),
+        (total.at[2 * LAT : 3 * LAT, :], out_msg),
+        (total.at[3 * LAT + 8 : 3 * LAT + 11, :], out_dec),
+    )
+    copies = [pltpu.make_async_copy(source, target, sems.at[n]) for n, (source, target) in enumerate(pairs)]
+    for copy in copies:
+        copy.start()
+    for copy in copies:
+        copy.wait()
 
 
 def per_device(sizes, scale, *args):
@@ -504,29 +558,42 @@
         cot_latent,
         cot_position,
     ) = args
-    slots = jnp.transpose(senders.reshape(OWN, NBR))
-    counts = nbr_count.reshape(1, OWN)
-    ghosts = jnp.stack([ghost_x.reshape(-1), ghost_y.reshape(-1), ghost_z.reshape(-1)])
+    given = (
+        latent,
+        position,
+        particle_count,
+        nbr_count.reshape(1, OWN),
+        senders.reshape(OWN * NBR // LAT, LAT),
+        ghost_x,
+        ghost_y,
+        ghost_z,
+        w_send,
+        w_recv,
+        w_geo,
+        w_msg,
+        w_dec,
+        cot_latent,
+        cot_position,
+    )
     nx, ny, nz = sizes
     piece_x = GRAD_ROWS // nx
     piece_y = piece_x // ny
     sums = 2 * (nx - 1) + 2 * (ny - 1) + (nz - 1)
     vmem = pl.BlockSpec(memory_space=pltpu.VMEM)
-    smem = pl.BlockSpec(memory_space=pltpu.SMEM)
-    return pl.pallas_call(
+    anywhere = pl.BlockSpec(memory_space=pl.ANY)
+    held = [(pltpu.SMEM if array.size == 1 else pltpu.VMEM)(array.shape, array.dtype) for array in given]
+    grad_x, grad_q, total = pl.pallas_call(
         functools.partial(kernel, sizes, scale),
         out_shape=(
             jax.ShapeDtypeStruct((OWN, LAT), F32),
             jax.ShapeDtypeStruct((3, OWN), F32),
-            jax.ShapeDtypeStruct((LAT, LAT), F32),
-            jax.ShapeDtypeStruct((LAT, LAT), F32),
-            jax.ShapeDtypeStruct((4, LAT), F32),
-            jax.ShapeDtypeStruct((LAT, LAT), F32),
-            jax.ShapeDtypeStruct((3, LAT), F32),
+            jax.ShapeDtypeStruct((GRAD_ROWS, LAT), F32),
         ),
-        in_specs=[vmem] * 5 + [smem] + [vmem] * 7,
-        out_specs=(vmem,) * 7,
+        in_specs=[pl.BlockSpec(memory_space=pltpu.HBM)] * INPUTS,
+        out_specs=(vmem,) * 3,
         scratch_shapes=[
+            *held,
+            pltpu.SemaphoreType.DMA((INPUTS,)),
             pltpu.VMEM((NBR, ROWS, OWN), BF16),
             pltpu.VMEM((OWN, GHOST), BF16),
             pltpu.VMEM((OWN + GHOST, GHOST), BF16),
@@ -556,33 +623,35 @@
             pltpu.VMEM((nz, piece_y, LAT), F32),
             pltpu.VMEM((nx - 1, piece_x, LAT), F32),
             pltpu.VMEM((ny - 1, piece_y, LAT), F32),
-            pltpu.VMEM((GRAD_ROWS, LAT), F32),
             pltpu.VMEM((12, 2, MSG, GHOST), F32),
             pltpu.VMEM((12, 2, MSG, GHOST), F32),
             pltpu.SemaphoreType.DMA((12, 2)),
             pltpu.SemaphoreType.DMA((12, 2)),
             pltpu.SemaphoreType.DMA((sums,)),
             pltpu.SemaphoreType.DMA((sums,)),
+            pltpu.VMEM((NBR, OWN), jnp.int32),
         ],
         compiler_params=pltpu.CompilerParams(
-            collective_id=0, has_side_effects=True, vmem_limit_bytes=48 * 1024 * 1024
+            collective_id=0, has_side_effects=True, vmem_limit_bytes=64 * 1024 * 1024
         ),
         name="evolver_backward",
-    )(
-        latent,
-        position,
-        slots,
-        counts,
-        ghosts,
-        particle_count,
-        w_send,
-        w_recv,
-        w_geo,
-        w_msg,
-        w_dec,
-        cot_latent,
-        cot_position,
-    )
+    )(*given)
+    return pl.pallas_call(
+        hand_out,
+        out_shape=(
+            jax.ShapeDtypeStruct((OWN, LAT), F32),
+            jax.ShapeDtypeStruct((3, OWN), F32),
+            jax.ShapeDtypeStruct((LAT, LAT), F32),
+            jax.ShapeDtypeStruct((LAT, LAT), F32),
+            jax.ShapeDtypeStruct((4, LAT), F32),
+            jax.ShapeDtypeStruct((LAT, LAT), F32),
+            jax.ShapeDtypeStruct((3, LAT), F32),
+        ),
+        in_specs=[vmem] * 3,
+        out_specs=(anywhere,) * 7,
+        scratch_shapes=[pltpu.SemaphoreType.DMA((7,))],
+        name="hand_out",
+    )(grad_x, grad_q, total)
 
 
 def solution(mesh):

time: 107 us -> 87.4 us (0.82)
  local copies, waits for them, and re-layouts: 10.5 us -> 0 us
  Pallas kernels: 94.9 us -> 85.9 us
    pallas_call x1, Pallas kernels: 94.9 us -> 84.1 us  [per_device(): pl.pallas_call(functools.partial(kernel, sizes, scale), out_shape=(jax.Sh...]
    unnamed x33 -> x0, local copies, waits for them, and re-layouts: 9.38 us -> none
    pallas_call x0 -> x1, Pallas kernels: none -> 1.81 us  [per_device(): pl.pallas_call(hand_out, out_shape=(jax.ShapeDtypeStruct((OWN, LAT), F32)...]
where the time goes in v2:
time: 87.4 us; the launch traced here: 87.2 us
  Pallas kernels  85.9 us (98%)
  between operations  1.29 us (1%)
    pallas_call x1, Pallas kernels, per_device(): pl.pallas_call(functools.partial(kernel, sizes, scale), out_shape=(jax.Sh...  84.1 us
    pallas_call x1, Pallas kernels, per_device(): pl.pallas_call(hand_out, out_shape=(jax.ShapeDtypeStruct((OWN, LAT), F32)...  1.81 us

profile of v2, /device:TPU:1, one launch (start us, length us, event | category | flops | bytes accessed | tf_op | source)
XLA Modules:
  0.0 87.2 jit_solution(8807542091606464065)
XLA Ops:
  1.3 84.1 %evolver_backward.1 = (f32[256,128]{1,0:T(8,128)}, f32[3,256]{1,0:T(4,128)}, f32[512,128]{1,0:T(8,128)}) custom-call(f32[256,128]{1,0:T(8,128)} %refs_0_.1, f32[3,256]{1,0:T(4,128)} %refs_1_.1, s32[1]{0:T(128)S(6)} %copy.22.refs_2_, s32[1,256]{1,0:T(1,128)} %bitcast.3, s32[32,128]{1,0:T(8,128)} %bitcast.2, s32[2,64]{1,0:T(2,128)} %refs_5_.1, ...), custom_call_target="tpu_custom_call" | custom-call | tf_op jit(solution)/shard_map/evolver_backward/pallas_call | solution.py:585
  85.4 1.8 %hand_out.1 = (f32[256,128]{1,0:T(8,128)}, f32[3,256]{1,0:T(4,128)}, f32[128,128]{1,0:T(8,128)}, f32[128,128]{1,0:T(8,128)}, f32[4,128]{1,0:T(4,128)}, /*index=5*/f32[128,128]{1,0:T(8,128)}, f32[3,128]{1,0:T(4,128)}) custom-call(f32[256,128]{1,0:T(8,128)} %get-tuple-element.10.grad_x, f32[3,256]{1,0:T(4,128)} %get-tuple-element.11.grad_q, ...), custom_call_target="tpu_custom_call" | custom-call | tf_op jit(solution)/shard_map/hand_out/pallas_call | solution.py:639

commit v3 on v2

--- a/solution.py
+++ b/solution.py
@@ -23,6 +23,8 @@
 MSG = SIDE + 8
 UNROLL = 8
 INPUTS = 15
+CORES = 2
+LOWS = 2
 
 
 def dot(left, right):
@@ -107,11 +109,10 @@
     w_geo_s,
     d_geo,
     grads,
-    part_x,
-    part_y,
-    part_z,
-    got_x,
-    got_y,
+    part_half,
+    part_ring,
+    got_core,
+    got_plane,
     send_buf,
     recv_buf,
     halo_send,
@@ -148,12 +149,28 @@
     sels = (sel_x, sel_y, sel_z)
 
     barrier = pltpu.get_barrier_semaphore()
-    partners = 0
-    for axis in range(3):
-        for k in range(1, sizes[axis]):
-            peer = lax.rem(index[axis] + k, sizes[axis])
-            pl.semaphore_signal(barrier, inc=1, device_id={AXES[axis]: peer}, device_id_type=MESH)
-            partners += 1
+    core, y = lax.rem(index[0], CORES), lax.div(index[0], CORES)
+    lows, xs = LOWS, sizes[1] // LOWS
+    x, low = lax.rem(index[1], xs), lax.div(index[1], xs)
+    plane, ring = sizes[0] // CORES * xs, sizes[2] * lows
+    at_plane, at_ring = y * xs + x, index[2] * lows + low
+
+    def plane_peer(k):
+        place = lax.rem(at_plane + k, plane)
+        return place, {"gx": lax.div(place, xs) * CORES + core, "gy": low * xs + lax.rem(place, xs)}
+
+    def ring_peer(k):
+        place = lax.rem(at_ring + k, ring)
+        return place, {"gy": lax.rem(place, lows) * xs + x, "gz": lax.div(place, lows)}
+
+    other_core = {"gx": y * CORES + 1 - core}
+    greeted = [plane_peer(k)[1] for k in range(1, plane)] + [ring_peer(k)[1] for k in range(1, ring)]
+    for axis in (0, 1):
+        for step in (1, sizes[axis] - 1):
+            greeted.append({AXES[axis]: lax.rem(index[axis] + step, sizes[axis])})
+    for peer in greeted:
+        pl.semaphore_signal(barrier, inc=1, device_id=peer, device_id_type=MESH)
+    partners = len(greeted)
 
     lane = lax.broadcasted_iota(jnp.int32, (SIDE, GHOST), 1)
     left = lane < SIDE
@@ -339,7 +356,10 @@
 
         start = OWN + 2 * GHOST
         d_send, d_q = scatter(start, GHOST)
-        copies = start_halo(phase, 2, exact(dot, w_send_ref[...], d_send), d_q)
+        if first:
+            copies = start_halo(phase, 2, exact(dot, w_send_ref[...], d_send), d_q)
+        else:
+            ghost_x, ghost_q = exact(dot, w_send_ref[...], d_send), d_q
         d_weight = exact(dot_nt, tab_x[step, :, start : start + GHOST], d_send)
         for start, width in ((OWN + GHOST, GHOST), (OWN, GHOST), (0, OWN)):
             d_send, d_q = scatter(start, width)
@@ -361,6 +381,9 @@
             else:
                 grads[base : base + rows, :] += piece
         tail(0)
+        if not first:
+            copies = start_halo(phase, 2, ghost_x, ghost_q)
+        tail(1)
 
         def arrived(number, axis, copies):
             field_x, field_q = end_halo(number, copies)
@@ -383,12 +406,13 @@
         copies = start_halo(phase + 1, 1, cot_x[:, start : start + GHOST], cot_q[:, start : start + GHOST])
         add(OWN, GHOST)
         add(0, OWN)
+        tail(2)
         add = arrived(phase + 1, 1, copies)
         start = OWN
         add(start, GHOST)
         copies = start_halo(phase + 2, 0, cot_x[:, start : start + GHOST], cot_q[:, start : start + GHOST])
         add(0, OWN)
-        tail(1)
+        tail(3)
         add = arrived(phase + 2, 0, copies)
         add(0, OWN)
         return cot_x[:, 0:OWN], cot_q[:, 0:OWN]
@@ -448,77 +472,68 @@
     pad[0:3, :] = cot_position_ref[...]
     cot_v, cot_p = backward(1, 6, jnp.transpose(cot_latent_ref[...]), pad[...], True, lambda number: None)
 
-    piece_x = GRAD_ROWS // sizes[0]
-    piece_y = piece_x // sizes[1]
-    bases = (0, sizes[0] - 1, sizes[0] + sizes[1] - 2)
-    more = bases[2] + sizes[2] - 1
-
-    def exchange(axis, base, source, target):
-        copies = []
-        for k in range(1, sizes[axis]):
-            peer = lax.rem(index[axis] + k, sizes[axis])
-            copy = pltpu.make_async_remote_copy(
-                src_ref=source(peer),
-                dst_ref=target(k),
-                send_sem=sum_send.at[base + k - 1],
-                recv_sem=sum_recv.at[base + k - 1],
-                device_id={AXES[axis]: peer},
-                device_id_type=MESH,
-            )
-            copy.start()
-            copies.append(copy)
-        pending.extend(copies)
-        return copies
-
-    state = {}
+    half = GRAD_ROWS // CORES
+    piece = half // plane
+    numbers = iter(range(2 + 2 * (plane - 1) + (ring - 1)))
+
+    def push(source, target, peer):
+        number = next(numbers)
+        copy = pltpu.make_async_remote_copy(
+            src_ref=source,
+            dst_ref=target,
+            send_sem=sum_send.at[number],
+            recv_sem=sum_recv.at[number],
+            device_id=peer,
+            device_id_type=MESH,
+        )
+        copy.start()
+        pending.append(copy)
+        return copy
+
+    def rows_of(base, count):
+        return pl.ds(pl.multiple_of(base, 8), count)
+
+    own_half = rows_of(core * half, half)
+    own_piece = rows_of(core * half + at_plane * piece, piece)
+    flying = []
+
+    def arrive():
+        for copy in flying:
+            copy.wait_recv()
+        flying.clear()
 
     def tail(number):
         if number == 0:
-            state["x"] = exchange(
-                0,
-                bases[0],
-                lambda peer: grads.at[pl.ds(pl.multiple_of(peer * piece_x, 8), piece_x), :],
-                lambda k: got_x.at[k - 1],
-            )
+            flying.append(push(grads.at[rows_of((1 - core) * half, half), :], got_core, other_core))
+        elif number == 1:
+            arrive()
+            part_half[...] = grads[own_half, :] + got_core[...]
+            for k in range(1, plane):
+                place, peer = plane_peer(k)
+                flying.append(push(part_half.at[rows_of(place * piece, piece), :], got_plane.at[k - 1], peer))
+        elif number == 2:
+            arrive()
+            value = part_half[rows_of(at_plane * piece, piece), :]
+            for k in range(plane - 1):
+                value = value + got_plane[k]
+            part_ring[at_ring] = value
+            for k in range(1, ring):
+                flying.append(push(part_ring.at[at_ring], part_ring.at[at_ring], ring_peer(k)[1]))
         else:
-            for copy in state["x"]:
-                copy.wait_recv()
-            value = grads[pl.ds(pl.multiple_of(index[0] * piece_x, 8), piece_x), :]
-            for k in range(sizes[0] - 1):
-                value = value + got_x[k]
-            part_x[...] = value
-            state["y"] = exchange(
-                1,
-                bases[1],
-                lambda peer: part_x.at[pl.ds(pl.multiple_of(peer * piece_y, 8), piece_y), :],
-                lambda k: got_y.at[k - 1],
-            )
+            arrive()
+            value = part_ring[0]
+            for k in range(1, ring):
+                value = value + part_ring[k]
+            total[own_piece, :] = value * scale
+            for k in range(1, plane):
+                flying.append(push(total.at[own_piece, :], total.at[own_piece, :], plane_peer(k)[1]))
 
     cot_v, cot_p = backward(0, 9, cot_v, cot_p, False, tail)
-    for copy in state["y"]:
-        copy.wait_recv()
-    value = part_x[pl.ds(pl.multiple_of(index[1] * piece_y, 8), piece_y), :]
-    for k in range(sizes[1] - 1):
-        value = value + got_y[k]
-    part_z[index[2]] = value
-    copies = exchange(2, bases[2], lambda peer: part_z.at[index[2]], lambda k: part_z.at[index[2]])
+    arrive()
+    flying.append(push(total.at[own_half, :], total.at[own_half, :], other_core))
     out_latent_ref[...] = jnp.transpose(cot_v)
     out_position_ref[...] = cot_p[0:3]
-    for copy in copies:
-        copy.wait_recv()
-    value = part_z[0]
-    for k in range(1, sizes[2]):
-        value = value + part_z[k]
-    own_y = pl.ds(pl.multiple_of(index[1] * piece_y, 8), piece_y)
-    part_y[own_y, :] = value * scale
-    copies = exchange(1, more, lambda peer: part_y.at[own_y, :], lambda k: part_y.at[own_y, :])
-    for copy in copies:
-        copy.wait_recv()
-    own_x = pl.ds(pl.multiple_of(index[0] * piece_x, 8), piece_x)
-    total[own_x, :] = part_y[...]
-    copies = exchange(0, more + sizes[1] - 1, lambda peer: part_y, lambda k: total.at[own_x, :])
-    for copy in copies:
-        copy.wait_recv()
+    arrive()
     for copy in pending:
         copy.wait_send()
 
@@ -575,10 +590,10 @@
         cot_latent,
         cot_position,
     )
-    nx, ny, nz = sizes
-    piece_x = GRAD_ROWS // nx
-    piece_y = piece_x // ny
-    sums = 2 * (nx - 1) + 2 * (ny - 1) + (nz - 1)
+    plane = sizes[0] // CORES * (sizes[1] // LOWS)
+    ring = sizes[2] * LOWS
+    half = GRAD_ROWS // CORES
+    sums = 2 + 2 * (plane - 1) + (ring - 1)
     vmem = pl.BlockSpec(memory_space=pltpu.VMEM)
     anywhere = pl.BlockSpec(memory_space=pl.ANY)
     held = [(pltpu.SMEM if array.size == 1 else pltpu.VMEM)(array.shape, array.dtype) for array in given]
@@ -618,11 +633,10 @@
             pltpu.VMEM((16, LAT), BF16),
             pltpu.VMEM((8, LAT), F32),
             pltpu.VMEM((GRAD_ROWS, LAT), F32),
-            pltpu.VMEM((piece_x, LAT), F32),
-            pltpu.VMEM((piece_x, LAT), F32),
-            pltpu.VMEM((nz, piece_y, LAT), F32),
-            pltpu.VMEM((nx - 1, piece_x, LAT), F32),
-            pltpu.VMEM((ny - 1, piece_y, LAT), F32),
+            pltpu.VMEM((half, LAT), F32),
+            pltpu.VMEM((ring, half // plane, LAT), F32),
+            pltpu.VMEM((half, LAT), F32),
+            pltpu.VMEM((plane - 1, half // plane, LAT), F32),
             pltpu.VMEM((12, 2, MSG, GHOST), F32),
             pltpu.VMEM((12, 2, MSG, GHOST), F32),
             pltpu.SemaphoreType.DMA((12, 2)),

time: 87.4 us -> 83.6 us (0.957)
  Pallas kernels: 85.9 us -> 82.2 us
    pallas_call x1, Pallas kernels: 84.1 us -> 80.4 us  [per_device(): pl.pallas_call(functools.partial(kernel, sizes, scale), out_shape=(jax.Sh...]
where the time goes in v3:
time: 83.6 us; the launch traced here: 83.5 us
  Pallas kernels  82.2 us (98%)
  between operations  1.29 us (2%)
    pallas_call x1, Pallas kernels, per_device(): pl.pallas_call(functools.partial(kernel, sizes, scale), out_shape=(jax.Sh...  80.4 us
    pallas_call x1, Pallas kernels, per_device(): pl.pallas_call(hand_out, out_shape=(jax.ShapeDtypeStruct((OWN, LAT), F32)...  1.81 us

profile of v3, /device:TPU:1, one launch (start us, length us, event | category | flops | bytes accessed | tf_op | source)
XLA Modules:
  0.0 83.5 jit_solution(6915913466454527158)
XLA Ops:
  1.3 80.4 %evolver_backward.1 = (f32[256,128]{1,0:T(8,128)}, f32[3,256]{1,0:T(4,128)}, f32[512,128]{1,0:T(8,128)}) custom-call(f32[256,128]{1,0:T(8,128)} %refs_0_.1, f32[3,256]{1,0:T(4,128)} %refs_1_.1, s32[1]{0:T(128)S(6)} %copy.22.refs_2_, s32[1,256]{1,0:T(1,128)} %bitcast.3, s32[32,128]{1,0:T(8,128)} %bitcast.2, s32[2,64]{1,0:T(2,128)} %refs_5_.1, ...), custom_call_target="tpu_custom_call" | custom-call | tf_op jit(solution)/shard_map/evolver_backward/pallas_call | solution.py:600
  81.7 1.8 %hand_out.1 = (f32[256,128]{1,0:T(8,128)}, f32[3,256]{1,0:T(4,128)}, f32[128,128]{1,0:T(8,128)}, f32[128,128]{1,0:T(8,128)}, f32[4,128]{1,0:T(4,128)}, /*index=5*/f32[128,128]{1,0:T(8,128)}, f32[3,128]{1,0:T(4,128)}) custom-call(f32[256,128]{1,0:T(8,128)} %get-tuple-element.10.grad_x, f32[3,256]{1,0:T(4,128)} %get-tuple-element.11.grad_q, ...), custom_call_target="tpu_custom_call" | custom-call | tf_op jit(solution)/shard_map/hand_out/pallas_call | solution.py:653

commit v4 on v3

--- a/solution.py
+++ b/solution.py
@@ -40,28 +40,40 @@
     return high, (value - high.astype(F32)).astype(BF16)
 
 
-def exact(product, left, right):
+def exact(left, right):
     left_high, left_low = split(left)
     right_high, right_low = split(right)
-    return product(left_high, right_high) + (product(left_low, right_high) + product(left_high, right_low))
-
-
-def split_rows(field_x, field_q):
-    high, low = split(field_x)
+    return dot(
+        jnp.concatenate([left_high, left_low, left_high], axis=1),
+        jnp.concatenate([right_high, right_high, right_low], axis=0),
+    )
+
+
+def exact_nt(left, right):
+    left_high, left_low = split(left)
+    right_high, right_low = split(right)
+    return dot_nt(
+        jnp.concatenate([left_high, left_low, left_high], axis=1),
+        jnp.concatenate([right_high, right_high, right_low], axis=1),
+    )
+
+
+def split_place(field_q):
     first = field_q.astype(BF16).astype(F32)
     rest = field_q - first
     second = rest.astype(BF16).astype(F32)
     third = rest - second
-    upper = jnp.concatenate([first, second], axis=0).astype(BF16)
-    lower = jnp.concatenate([third, jnp.zeros_like(third)], axis=0).astype(BF16)
-    return high, low, upper, lower
+    left = jnp.concatenate([first, third], axis=0).astype(BF16)
+    right = jnp.concatenate([second, jnp.zeros_like(third)], axis=0).astype(BF16)
+    return left, right
+
+
+def twice(picker):
+    return jnp.concatenate([picker, picker], axis=0)
 
 
 def join_rows(product):
-    value = product[0:LAT] + product[LAT : 2 * LAT]
-    base = 2 * LAT
-    place = product[base : base + 8] + product[base + 8 : base + 16] + product[base + 16 : base + 24]
-    return value, place
+    return product[0:LAT], product[LAT : LAT + 8] + product[LAT + 8 : LAT + 16]
 
 
 def kernel(
@@ -89,9 +101,15 @@
     sel_x,
     sel_y,
     sel_z,
+    back_x,
+    back_y,
+    back_z,
+    edge_rows,
+    edge_sum,
     tab_x,
     tab_q,
     tab_s,
+    tab_w,
     tab_a,
     gath,
     slope,
@@ -107,7 +125,6 @@
     w_t,
     w_geo_k,
     w_geo_s,
-    d_geo,
     grads,
     part_half,
     part_ring,
@@ -147,6 +164,7 @@
         load.start()
     index = tuple(lax.axis_index(axis) for axis in AXES)
     sels = (sel_x, sel_y, sel_z)
+    backs = (back_x, back_y, back_z)
 
     barrier = pltpu.get_barrier_semaphore()
     core, y = lax.rem(index[0], CORES), lax.div(index[0], CORES)
@@ -186,7 +204,12 @@
         lists = ghost_refs[axis][...]
         chosen = jnp.concatenate([lists[0:1], lists[1:2]], axis=1)
         ids = lax.broadcasted_iota(jnp.int32, (rows, GHOST), 0)
-        sels[axis][...] = (ids == chosen).astype(F32).astype(BF16)
+        picked = (ids == chosen).astype(F32)
+        sels[axis][...] = picked.astype(BF16)
+        return picked
+
+    def edges_of(n):
+        return pl.ds(pl.multiple_of(n * OWN, OWN), OWN)
 
     pending = []
 
@@ -229,21 +252,22 @@
         cols = slice(start, start + width)
         tab_x[step, :, cols] = field_x
         tab_q[step, :, cols] = field_q
-        high, low, upper, lower = split_rows(field_x, field_q)
-        tab_s[0:LAT, cols] = high
-        tab_s[LAT : 2 * LAT, cols] = low
-        tab_s[256:272, cols] = upper
-        tab_s[272:288, cols] = lower
+        left, right = slice(2 * start, 2 * start + width), slice(2 * start + width, 2 * start + 2 * width)
+        high, low = split(field_x)
+        tab_s[0:LAT, left] = high
+        tab_s[0:LAT, right] = low
+        tab_w[step, 0:LAT, cols] = high
+        tab_w[step, LAT:, cols] = low
+        tab_s[LAT:, left], tab_s[LAT:, right] = split_place(field_q)
 
     def project_block(step, start, width):
-        cols = slice(start, start + width)
-        high, low = split(exact(dot, w_t[0], tab_x[step, :, cols]))
-        tab_a[0:LAT, cols] = high
-        tab_a[LAT : 2 * LAT, cols] = low
-        tab_a[256:288, cols] = tab_s[256:288, cols]
+        cols = slice(2 * start, 2 * start + 2 * width)
+        high, low = split(exact(w_t[0], tab_x[step, :, start : start + width]))
+        tab_a[0:LAT, cols] = jnp.concatenate([high, low], axis=1)
+        tab_a[LAT:, cols] = tab_s[LAT:, cols]
 
     def select(axis, start, width):
-        return dot(tab_s[:, start : start + width], sels[axis][start : start + width, :])
+        return dot(tab_s[:, 2 * start : 2 * (start + width)], twice(sels[axis][start : start + width, :]))
 
     def send_rows(phase, axis, product):
         field_x, field_q = join_rows(product)
@@ -254,7 +278,8 @@
 
     def gather_block(start, width, extra=None):
         def body(n, carry):
-            value, place = join_rows(dot(tab_a[:, start : start + width], onehot[n, start : start + width, :]))
+            picker = twice(onehot[n, start : start + width, :])
+            value, place = join_rows(dot(tab_a[:, 2 * start : 2 * (start + width)], picker))
             if extra is None:
                 gath[n, 0:LAT, :] += value
                 gath[n, LAT:, :] += place
@@ -269,7 +294,7 @@
         copies = send_rows(phase, 0, select(0, 0, OWN))
         prologue()
         project_block(step, 0, OWN)
-        d_recv[...] = exact(dot, w_t[1], tab_x[step, :, 0:OWN])
+        d_recv[...] = exact(w_t[1], tab_x[step, :, 0:OWN])
         early_y = select(1, 0, OWN)
         early_z = select(2, 0, OWN)
         gather_block(0, OWN, d_recv)
@@ -292,7 +317,8 @@
         summed[step] = jnp.zeros((LAT, OWN), F32)
 
         def body(n, carry):
-            value, place = join_rows(dot(tab_a[:, start : start + GHOST], onehot[n, start : start + GHOST, :]))
+            picker = twice(onehot[n, start : start + GHOST, :])
+            value, place = join_rows(dot(tab_a[:, 2 * start : 2 * (start + GHOST)], picker))
             rel = gath[n, LAT:, :] + place - own_q
             dist = jnp.sum(rel * rel, axis=0, keepdims=True)
             geo = jnp.where(row8_own == 3, dist, rel)
@@ -300,6 +326,7 @@
             coarse = geo.astype(BF16).astype(F32)
             fine = geo - coarse
             rows = jnp.concatenate([coarse, fine, coarse, jnp.zeros_like(fine)], axis=0).astype(BF16)
+            edge_rows[step, 2 * LAT :, edges_of(n)] = rows[0:16]
             pre = gath[n, 0:LAT, :] + value + dot(w_geo_k[...], rows)
             gate = 0.5 * jnp.tanh(0.5 * pre) + 0.5
             keep = (counts > n).astype(F32)
@@ -309,16 +336,23 @@
             return carry
 
         lax.fori_loop(0, NBR, body, 0, unroll=UNROLL)
-        new_x = tab_x[step, :, 0:OWN] + live * exact(dot, w_t[2], summed[step])
+        new_x = tab_x[step, :, 0:OWN] + live * exact(w_t[2], summed[step])
         fresh[step] = new_x
         return new_x
 
     def scatter(start, width):
         def body(n, carry):
-            return carry + dot_nt(dpre[n], onehot[n, start : start + width, :])
-
-        product = lax.fori_loop(0, NBR, body, jnp.zeros((272, width), F32), unroll=UNROLL)
+            return carry + dot_nt(dpre[:, edges_of(n)], onehot[n, start : start + width, :])
+
+        product = lax.fori_loop(0, NBR, body, jnp.zeros((2 * LAT + 16, width), F32), unroll=UNROLL)
         return product[0:LAT] + product[LAT : 2 * LAT], product[256:264] + product[264:272]
+
+    def gather_latents(step):
+        def body(n, carry):
+            edge_rows[step, 0 : 2 * LAT, edges_of(n)] = dot(tab_w[step], onehot[n]).astype(BF16)
+            return carry
+
+        lax.fori_loop(0, NBR, body, 0, unroll=UNROLL)
 
     def backward(step, phase, cot_v, cot_p, first, tail):
         move = STRIDE * live * cot_p
@@ -326,77 +360,82 @@
         for k in range(3):
             full = full + w_t[3, :, k : k + 1] * move[k : k + 1, :]
         d_agg = live * full
-        d_sum = exact(dot, w_msg_ref[...], d_agg)
+        d_sum = exact(w_msg_ref[...], d_agg)
         d_recv[...] = jnp.zeros((LAT, OWN), F32)
         d_place[...] = jnp.zeros((8, OWN), F32)
-        d_geo[...] = jnp.zeros((8, LAT), F32)
 
         def body(n, carry):
             value = d_sum * slope[step, n]
             geo = geos[step, n]
             high, low = split(value)
-            dpre[n, 0:LAT, :] = high
-            dpre[n, LAT : 2 * LAT, :] = low
+            cols = edges_of(n)
+            dpre[0:LAT, cols] = high
+            dpre[LAT : 2 * LAT, cols] = low
             d_recv[...] += value
-            main = dot(w_geo_s[...], high)
-            side = dot(w_geo_s[...], low)
-            back = main[0:8] + main[8:16] + side[0:8]
+            back = dot(w_geo_s[...], jnp.concatenate([high, low], axis=0))
+            back = back[0:8] + back[8:16]
             d_rel = jnp.where(row8_own < 3, back + 2.0 * geo * back[3:4], 0.0)
             d_place[...] -= d_rel
             coarse = d_rel.astype(BF16).astype(F32)
-            dpre[n, 256:272, :] = jnp.concatenate([coarse, d_rel - coarse], axis=0).astype(BF16)
-            geo_high = geo.astype(BF16).astype(F32)
-            geo_rows = jnp.concatenate([geo_high, geo - geo_high], axis=0).astype(BF16)
-            main = dot_nt(geo_rows, high)
-            side = dot_nt(geo_rows, low)
-            d_geo[...] += main[0:8] + main[8:16] + side[0:8]
+            dpre[2 * LAT :, cols] = jnp.concatenate([coarse, d_rel - coarse], axis=0).astype(BF16)
             return carry
 
         lax.fori_loop(0, NBR, body, 0, unroll=UNROLL)
 
-        start = OWN + 2 * GHOST
-        d_send, d_q = scatter(start, GHOST)
+        def spread(start, width):
+            d_send, d_q = scatter(start, width)
+            return exact(w_send_ref[...], d_send), d_q
+
+        def spread_block(start, width):
+            cot_x[:, start : start + width], cot_q[:, start : start + width] = spread(start, width)
+
+        def weights(d_weight, d_geo):
+            pieces = (
+                (0, LAT, d_weight),
+                (LAT, LAT, exact_nt(tab_x[step, :, 0:OWN], d_recv[...])),
+                (2 * LAT, LAT, exact_nt(summed[step], d_agg)),
+                (3 * LAT, 8, d_geo),
+                (3 * LAT + 8, 8, exact_nt(move, fresh[step])),
+            )
+            for base, rows, piece in pieces:
+                if first:
+                    grads[base : base + rows, :] = piece
+                else:
+                    grads[base : base + rows, :] += piece
+
+        def by_edges():
+            edge_sum[...] = jnp.zeros((2 * LAT + 16, 2 * LAT), F32)
+
+            def body(n, carry):
+                edge_sum[...] += dot_nt(edge_rows[step, :, edges_of(n)], dpre[0 : 2 * LAT, edges_of(n)])
+                return carry
+
+            lax.fori_loop(0, NBR, body, 0, unroll=UNROLL)
+            product = edge_sum[...]
+            geo = product[256:264, 0:LAT] + product[256:264, LAT:] + product[264:272, 0:LAT]
+            return product[0:LAT, 0:LAT] + product[0:LAT, LAT:] + product[LAT : 2 * LAT, 0:LAT], geo
+
+        if not first:
+            weights(*by_edges())
+            tail(0)
+        copies = start_halo(phase, 2, *spread(OWN + 2 * GHOST, GHOST))
+        tail(1)
+        spread_block(OWN + GHOST, GHOST)
         if first:
-            copies = start_halo(phase, 2, exact(dot, w_send_ref[...], d_send), d_q)
-        else:
-            ghost_x, ghost_q = exact(dot, w_send_ref[...], d_send), d_q
-        d_weight = exact(dot_nt, tab_x[step, :, start : start + GHOST], d_send)
-        for start, width in ((OWN + GHOST, GHOST), (OWN, GHOST), (0, OWN)):
-            d_send, d_q = scatter(start, width)
-            cot_x[:, start : start + width] = exact(dot, w_send_ref[...], d_send)
-            cot_q[:, start : start + width] = d_q
-            d_weight = d_weight + exact(dot_nt, tab_x[step, :, start : start + width], d_send)
-        cot_x[:, 0:OWN] += full + exact(dot, w_recv_ref[...], d_recv[...])
-        cot_q[:, 0:OWN] += cot_p + d_place[...]
-        pieces = (
-            (0, LAT, d_weight),
-            (LAT, LAT, exact(dot_nt, tab_x[step, :, 0:OWN], d_recv[...])),
-            (2 * LAT, LAT, exact(dot_nt, summed[step], d_agg)),
-            (3 * LAT, 8, d_geo[...]),
-            (3 * LAT + 8, 8, exact(dot_nt, move, fresh[step])),
-        )
-        for base, rows, piece in pieces:
-            if first:
-                grads[base : base + rows, :] = piece
-            else:
-                grads[base : base + rows, :] += piece
-        tail(0)
-        if not first:
-            copies = start_halo(phase, 2, ghost_x, ghost_q)
-        tail(1)
+            gather_latents(1)
 
         def arrived(number, axis, copies):
             field_x, field_q = end_halo(number, copies)
             high, low = split(field_x)
-            coarse = field_q.astype(BF16).astype(F32)
-            rows = jnp.concatenate([coarse, field_q - coarse], axis=0).astype(BF16)
+            left, right = split_place(field_q)
+            rows = jnp.concatenate(
+                [jnp.concatenate([high, low], axis=1), jnp.concatenate([left, right], axis=1)], axis=0
+            )
 
             def add(start, width):
-                sel = sels[axis][start : start + width, :]
-                extra = dot_nt(high, sel) + dot_nt(low, sel)
-                extra_q = dot_nt(rows, sel)
+                extra, extra_q = join_rows(dot(rows, twice(backs[axis][:, start : start + width])))
                 cot_x[:, start : start + width] += extra
-                cot_q[:, start : start + width] += extra_q[0:8] + extra_q[8:16]
+                cot_q[:, start : start + width] += extra_q
 
             return add
 
@@ -404,15 +443,22 @@
         start = OWN + GHOST
         add(start, GHOST)
         copies = start_halo(phase + 1, 1, cot_x[:, start : start + GHOST], cot_q[:, start : start + GHOST])
+        tail(2)
+        spread_block(OWN, GHOST)
+        spread_block(0, OWN)
+        cot_x[:, 0:OWN] += full + exact(w_recv_ref[...], d_recv[...])
+        cot_q[:, 0:OWN] += cot_p + d_place[...]
         add(OWN, GHOST)
         add(0, OWN)
-        tail(2)
         add = arrived(phase + 1, 1, copies)
         start = OWN
         add(start, GHOST)
         copies = start_halo(phase + 2, 0, cot_x[:, start : start + GHOST], cot_q[:, start : start + GHOST])
+        tail(3)
         add(0, OWN)
-        tail(3)
+        if first:
+            weights(*by_edges())
+            gather_latents(0)
         add = arrived(phase + 2, 0, copies)
         add(0, OWN)
         return cot_x[:, 0:OWN], cot_q[:, 0:OWN]
@@ -424,8 +470,8 @@
     pl.semaphore_wait(barrier, partners)
 
     def prologue():
-        selector(1)
-        selector(2)
+        for axis in range(3):
+            backs[axis][...] = jnp.transpose(selector(axis)).astype(BF16)
         w_t[0] = jnp.transpose(w_send_ref[...])
         w_t[1] = jnp.transpose(w_recv_ref[...])
         w_t[2] = jnp.transpose(w_msg_ref[...])
@@ -437,7 +483,9 @@
         w_geo = w_t[4, 0:8, :]
         coarse = w_geo.astype(BF16).astype(F32)
         fine = w_geo - coarse
-        w_geo_s[...] = jnp.concatenate([coarse, fine], axis=0).astype(BF16)
+        main = jnp.concatenate([coarse, fine], axis=0)
+        side = jnp.concatenate([coarse, jnp.zeros_like(fine)], axis=0)
+        w_geo_s[...] = jnp.concatenate([main, side], axis=1).astype(BF16)
         w_t[4, 0:8, :] = coarse
         w_t[4, 8:16, :] = coarse
         w_t[4, 16:24, :] = fine
@@ -465,7 +513,7 @@
 
     new_x = forward(0, 0, prologue)
     w_dec = jnp.concatenate([w_dec_ref[...], jnp.zeros((5, LAT), F32)], axis=0)
-    new_q = tab_q[0, :, 0:OWN] + STRIDE * live * exact(dot, w_dec, new_x)
+    new_q = tab_q[0, :, 0:OWN] + STRIDE * live * exact(w_dec, new_x)
     set_block(1, 0, OWN, new_x, new_q)
     forward(1, 3, lambda: None)
 
@@ -613,16 +661,22 @@
             pltpu.VMEM((OWN, GHOST), BF16),
             pltpu.VMEM((OWN + GHOST, GHOST), BF16),
             pltpu.VMEM((OWN + 2 * GHOST, GHOST), BF16),
+            pltpu.VMEM((GHOST, OWN), BF16),
+            pltpu.VMEM((GHOST, OWN + GHOST), BF16),
+            pltpu.VMEM((GHOST, OWN + 2 * GHOST), BF16),
+            pltpu.VMEM((2, 2 * LAT + 16, NBR * OWN), BF16),
+            pltpu.VMEM((2 * LAT + 16, 2 * LAT), F32),
             pltpu.VMEM((2, LAT, ROWS), F32),
             pltpu.VMEM((2, 8, ROWS), F32),
-            pltpu.VMEM((288, ROWS), BF16),
-            pltpu.VMEM((288, ROWS), BF16),
+            pltpu.VMEM((LAT + 16, 2 * ROWS), BF16),
+            pltpu.VMEM((2, 2 * LAT, ROWS), BF16),
+            pltpu.VMEM((LAT + 16, 2 * ROWS), BF16),
             pltpu.VMEM((NBR, LAT + 8, OWN), F32),
             pltpu.VMEM((2, NBR, LAT, OWN), F32),
             pltpu.VMEM((2, NBR, 8, OWN), F32),
             pltpu.VMEM((2, LAT, OWN), F32),
             pltpu.VMEM((2, LAT, OWN), F32),
-            pltpu.VMEM((NBR, 272, OWN), BF16),
+            pltpu.VMEM((2 * LAT + 16, NBR * OWN), BF16),
             pltpu.VMEM((LAT, OWN), F32),
             pltpu.VMEM((8, OWN), F32),
             pltpu.VMEM((LAT, ROWS), F32),
@@ -630,8 +684,7 @@
             pltpu.VMEM((8, OWN), F32),
             pltpu.VMEM((5, LAT, LAT), F32),
             pltpu.VMEM((LAT, 32), BF16),
-            pltpu.VMEM((16, LAT), BF16),
-            pltpu.VMEM((8, LAT), F32),
+            pltpu.VMEM((16, 2 * LAT), BF16),
             pltpu.VMEM((GRAD_ROWS, LAT), F32),
             pltpu.VMEM((half, LAT), F32),
             pltpu.VMEM((ring, half // plane, LAT), F32),

time: 83.6 us -> 80.3 us (0.961)
  Pallas kernels: 82.2 us -> 78.9 us
    pallas_call x1, Pallas kernels: 80.4 us -> 77.1 us  [per_device(): pl.pallas_call(functools.partial(kernel, sizes, scale), out_shape=(jax.Sh...]
where the time goes in v4:
time: 80.3 us; the launch traced here: 80.2 us
  Pallas kernels  78.9 us (98%)
  between operations  1.29 us (2%)
    pallas_call x1, Pallas kernels, per_device(): pl.pallas_call(functools.partial(kernel, sizes, scale), out_shape=(jax.Sh...  77.1 us
    pallas_call x1, Pallas kernels, per_device(): pl.pallas_call(hand_out, out_shape=(jax.ShapeDtypeStruct((OWN, LAT), F32)...  1.81 us

profile of v4, /device:TPU:1, one launch (start us, length us, event | category | flops | bytes accessed | tf_op | source)
XLA Modules:
  0.0 80.2 jit_solution(5921684102598580580)
XLA Ops:
  1.3 77.1 %evolver_backward.1 = (f32[256,128]{1,0:T(8,128)}, f32[3,256]{1,0:T(4,128)}, f32[512,128]{1,0:T(8,128)}) custom-call(f32[256,128]{1,0:T(8,128)} %refs_0_.1, f32[3,256]{1,0:T(4,128)} %refs_1_.1, s32[1]{0:T(128)S(6)} %copy.22.refs_2_, s32[1,256]{1,0:T(1,128)} %bitcast.3, s32[32,128]{1,0:T(8,128)} %bitcast.2, s32[2,64]{1,0:T(2,128)} %refs_5_.1, ...), custom_call_target="tpu_custom_call" | custom-call | tf_op jit(solution)/shard_map/evolver_backward/pallas_call | solution.py:648
  78.4 1.8 %hand_out.1 = (f32[256,128]{1,0:T(8,128)}, f32[3,256]{1,0:T(4,128)}, f32[128,128]{1,0:T(8,128)}, f32[128,128]{1,0:T(8,128)}, f32[4,128]{1,0:T(4,128)}, /*index=5*/f32[128,128]{1,0:T(8,128)}, f32[3,128]{1,0:T(4,128)}) custom-call(f32[256,128]{1,0:T(8,128)} %get-tuple-element.10.grad_x, f32[3,256]{1,0:T(4,128)} %get-tuple-element.11.grad_q, ...), custom_call_target="tpu_custom_call" | custom-call | tf_op jit(solution)/shard_map/hand_out/pallas_call | solution.py:706

commit v5 on v4

--- a/solution.py
+++ b/solution.py
@@ -106,6 +106,10 @@
     back_z,
     edge_rows,
     edge_sum,
+    moved,
+    fulls,
+    d_sum,
+    d_back,
     tab_x,
     tab_q,
     tab_s,
@@ -160,8 +164,6 @@
         pltpu.make_async_copy(source, target, load_sem.at[number])
         for number, (source, target) in enumerate(zip(given, held))
     ]
-    for load in loads:
-        load.start()
     index = tuple(lax.axis_index(axis) for axis in AXES)
     sels = (sel_x, sel_y, sel_z)
     backs = (back_x, back_y, back_z)
@@ -189,14 +191,18 @@
     for peer in greeted:
         pl.semaphore_signal(barrier, inc=1, device_id=peer, device_id_type=MESH)
     partners = len(greeted)
+    early = (0, 1, 2, 5, 6, 7)
+    order = early + tuple(number for number in range(INPUTS) if number not in early)
+    for number in order:
+        loads[number].start()
 
     lane = lax.broadcasted_iota(jnp.int32, (SIDE, GHOST), 1)
     left = lane < SIDE
     left8 = left[0:8]
     row8 = lax.broadcasted_iota(jnp.int32, (8, GHOST), 0)
     row8_own = lax.broadcasted_iota(jnp.int32, (8, OWN), 0)
-    for load in loads:
-        load.wait()
+    for number in early:
+        loads[number].wait()
     live = (lax.broadcasted_iota(jnp.int32, (1, OWN), 1) < particles_ref[0]).astype(F32)
 
     def selector(axis):
@@ -224,6 +230,8 @@
         lower = lax.rem(index[axis] + size - 1, size)
         upper = lax.rem(index[axis] + 1, size)
         copies = []
+        if phase == 0:
+            pl.semaphore_wait(barrier, partners)
         for side, peer in ((0, lower), (1, upper)):
             copy = pltpu.make_async_remote_copy(
                 src_ref=send_buf.at[phase, side],
@@ -290,7 +298,33 @@
 
         lax.fori_loop(0, NBR, body, 0, unroll=UNROLL)
 
-    def forward(step, phase, prologue):
+    def prepare(cot_v, cot_p):
+        move = STRIDE * live * cot_p
+        full = cot_v
+        for k in range(3):
+            full = full + w_t[3, :, k : k + 1] * move[k : k + 1, :]
+        d_agg = live * full
+        moved[...] = move
+        fulls[...] = full
+        d_sum[...] = exact(w_msg_ref[...], d_agg)
+        d_back[...] = jnp.zeros((LAT, OWN), F32)
+        d_place[...] = jnp.zeros((8, OWN), F32)
+
+    def push_back(n, slope_n, geo):
+        value = d_sum[...] * slope_n
+        high, low = split(value)
+        cols = edges_of(n)
+        dpre[0:LAT, cols] = high
+        dpre[LAT : 2 * LAT, cols] = low
+        d_back[...] += value
+        back = dot(w_geo_s[...], jnp.concatenate([high, low], axis=0))
+        back = back[0:8] + back[8:16]
+        d_rel = jnp.where(row8_own < 3, back + 2.0 * geo * back[3:4], 0.0)
+        d_place[...] -= d_rel
+        coarse = d_rel.astype(BF16).astype(F32)
+        dpre[2 * LAT :, cols] = jnp.concatenate([coarse, d_rel - coarse], axis=0).astype(BF16)
+
+    def forward(step, phase, prologue, beside):
         copies = send_rows(phase, 0, select(0, 0, OWN))
         prologue()
         project_block(step, 0, OWN)
@@ -298,6 +332,7 @@
         early_y = select(1, 0, OWN)
         early_z = select(2, 0, OWN)
         gather_block(0, OWN, d_recv)
+        beside()
         start = OWN
         set_block(step, start, GHOST, *end_halo(phase, copies))
         copies = send_rows(phase + 1, 1, early_y + select(1, start, GHOST))
@@ -317,16 +352,21 @@
         summed[step] = jnp.zeros((LAT, OWN), F32)
 
         def body(n, carry):
-            picker = twice(onehot[n, start : start + GHOST, :])
-            value, place = join_rows(dot(tab_a[:, 2 * start : 2 * (start + GHOST)], picker))
-            rel = gath[n, LAT:, :] + place - own_q
+            product = dot(tab_a[LAT:, 2 * start : 2 * (start + GHOST)], twice(onehot[n, start : start + GHOST, :]))
+            rel = gath[n, LAT:, :] + (product[0:8] + product[8:16]) - own_q
             dist = jnp.sum(rel * rel, axis=0, keepdims=True)
             geo = jnp.where(row8_own == 3, dist, rel)
             geos[step, n] = geo
             coarse = geo.astype(BF16).astype(F32)
-            fine = geo - coarse
-            rows = jnp.concatenate([coarse, fine, coarse, jnp.zeros_like(fine)], axis=0).astype(BF16)
-            edge_rows[step, 2 * LAT :, edges_of(n)] = rows[0:16]
+            edge_rows[step, 2 * LAT :, edges_of(n)] = jnp.concatenate([coarse, geo - coarse], axis=0).astype(BF16)
+            return carry
+
+        lax.fori_loop(0, NBR, body, 0, unroll=UNROLL)
+
+        def body(n, carry):
+            picker = twice(onehot[n, start : start + GHOST, :])
+            value = dot(tab_a[0:LAT, 2 * start : 2 * (start + GHOST)], picker)
+            rows = twice(edge_rows[step, 2 * LAT :, edges_of(n)])
             pre = gath[n, 0:LAT, :] + value + dot(w_geo_k[...], rows)
             gate = 0.5 * jnp.tanh(0.5 * pre) + 0.5
             keep = (counts > n).astype(F32)
@@ -336,6 +376,8 @@
             return carry
 
         lax.fori_loop(0, NBR, body, 0, unroll=UNROLL)
+
+    def update(step):
         new_x = tab_x[step, :, 0:OWN] + live * exact(w_t[2], summed[step])
         fresh[step] = new_x
         return new_x
@@ -355,29 +397,11 @@
         lax.fori_loop(0, NBR, body, 0, unroll=UNROLL)
 
     def backward(step, phase, cot_v, cot_p, first, tail):
-        move = STRIDE * live * cot_p
-        full = cot_v
-        for k in range(3):
-            full = full + w_t[3, :, k : k + 1] * move[k : k + 1, :]
-        d_agg = live * full
-        d_sum = exact(w_msg_ref[...], d_agg)
-        d_recv[...] = jnp.zeros((LAT, OWN), F32)
-        d_place[...] = jnp.zeros((8, OWN), F32)
+        if not first:
+            prepare(cot_v, cot_p)
 
         def body(n, carry):
-            value = d_sum * slope[step, n]
-            geo = geos[step, n]
-            high, low = split(value)
-            cols = edges_of(n)
-            dpre[0:LAT, cols] = high
-            dpre[LAT : 2 * LAT, cols] = low
-            d_recv[...] += value
-            back = dot(w_geo_s[...], jnp.concatenate([high, low], axis=0))
-            back = back[0:8] + back[8:16]
-            d_rel = jnp.where(row8_own < 3, back + 2.0 * geo * back[3:4], 0.0)
-            d_place[...] -= d_rel
-            coarse = d_rel.astype(BF16).astype(F32)
-            dpre[2 * LAT :, cols] = jnp.concatenate([coarse, d_rel - coarse], axis=0).astype(BF16)
+            push_back(n, slope[step, n], geos[step, n])
             return carry
 
         lax.fori_loop(0, NBR, body, 0, unroll=UNROLL)
@@ -390,12 +414,14 @@
             cot_x[:, start : start + width], cot_q[:, start : start + width] = spread(start, width)
 
         def weights(d_weight, d_geo):
+            if first:
+                update(step)
             pieces = (
                 (0, LAT, d_weight),
-                (LAT, LAT, exact_nt(tab_x[step, :, 0:OWN], d_recv[...])),
-                (2 * LAT, LAT, exact_nt(summed[step], d_agg)),
+                (LAT, LAT, exact_nt(tab_x[step, :, 0:OWN], d_back[...])),
+                (2 * LAT, LAT, exact_nt(summed[step], live * fulls[...])),
                 (3 * LAT, 8, d_geo),
-                (3 * LAT + 8, 8, exact_nt(move, fresh[step])),
+                (3 * LAT + 8, 8, exact_nt(moved[...], fresh[step])),
             )
             for base, rows, piece in pieces:
                 if first:
@@ -446,7 +472,7 @@
         tail(2)
         spread_block(OWN, GHOST)
         spread_block(0, OWN)
-        cot_x[:, 0:OWN] += full + exact(w_recv_ref[...], d_recv[...])
+        cot_x[:, 0:OWN] += fulls[...] + exact(w_recv_ref[...], d_back[...])
         cot_q[:, 0:OWN] += cot_p + d_place[...]
         add(OWN, GHOST)
         add(0, OWN)
@@ -467,9 +493,10 @@
     pad[0:3, :] = position_ref[...]
     set_block(0, 0, OWN, jnp.transpose(latent_ref[...]), pad[...])
     selector(0)
-    pl.semaphore_wait(barrier, partners)
 
     def prologue():
+        for number in order[len(early) :]:
+            loads[number].wait()
         for axis in range(3):
             backs[axis][...] = jnp.transpose(selector(axis)).astype(BF16)
         w_t[0] = jnp.transpose(w_send_ref[...])
@@ -511,14 +538,18 @@
 
         lax.fori_loop(0, NBR, body, 0)
 
-    new_x = forward(0, 0, prologue)
+    forward(0, 0, prologue, lambda: None)
+    new_x = update(0)
     w_dec = jnp.concatenate([w_dec_ref[...], jnp.zeros((5, LAT), F32)], axis=0)
     new_q = tab_q[0, :, 0:OWN] + STRIDE * live * exact(w_dec, new_x)
     set_block(1, 0, OWN, new_x, new_q)
-    forward(1, 3, lambda: None)
-
-    pad[0:3, :] = cot_position_ref[...]
-    cot_v, cot_p = backward(1, 6, jnp.transpose(cot_latent_ref[...]), pad[...], True, lambda number: None)
+
+    def beside():
+        pad[0:3, :] = cot_position_ref[...]
+        prepare(jnp.transpose(cot_latent_ref[...]), pad[...])
+
+    forward(1, 3, lambda: None, beside)
+    cot_v, cot_p = backward(1, 6, None, pad[...], True, lambda number: None)
 
     half = GRAD_ROWS // CORES
     piece = half // plane
@@ -666,6 +697,10 @@
             pltpu.VMEM((GHOST, OWN + 2 * GHOST), BF16),
             pltpu.VMEM((2, 2 * LAT + 16, NBR * OWN), BF16),
             pltpu.VMEM((2 * LAT + 16, 2 * LAT), F32),
+            pltpu.VMEM((8, OWN), F32),
+            pltpu.VMEM((LAT, OWN), F32),
+            pltpu.VMEM((LAT, OWN), F32),
+            pltpu.VMEM((LAT, OWN), F32),
             pltpu.VMEM((2, LAT, ROWS), F32),
             pltpu.VMEM((2, 8, ROWS), F32),
             pltpu.VMEM((LAT + 16, 2 * ROWS), BF16),

time: 80.3 us -> 78.3 us (0.975)
  Pallas kernels: 78.9 us -> 76.9 us
    pallas_call x1, Pallas kernels: 77.1 us -> 75.1 us  [per_device(): pl.pallas_call(functools.partial(kernel, sizes, scale), out_shape=(jax.Sh...]
where the time goes in v5:
time: 78.3 us; the launch traced here: 78.2 us
  Pallas kernels  76.9 us (98%)
  between operations  1.29 us (2%)
    pallas_call x1, Pallas kernels, per_device(): pl.pallas_call(functools.partial(kernel, sizes, scale), out_shape=(jax.Sh...  75.1 us
    pallas_call x1, Pallas kernels, per_device(): pl.pallas_call(hand_out, out_shape=(jax.ShapeDtypeStruct((OWN, LAT), F32)...  1.81 us

profile of v5, /device:TPU:1, one launch (start us, length us, event | category | flops | bytes accessed | tf_op | source)
XLA Modules:
  0.0 78.2 jit_solution(7152306159865503999)
XLA Ops:
  1.3 75.1 %evolver_backward.1 = (f32[256,128]{1,0:T(8,128)}, f32[3,256]{1,0:T(4,128)}, f32[512,128]{1,0:T(8,128)}) custom-call(f32[256,128]{1,0:T(8,128)} %refs_0_.1, f32[3,256]{1,0:T(4,128)} %refs_1_.1, s32[1]{0:T(128)S(6)} %copy.22.refs_2_, s32[1,256]{1,0:T(1,128)} %bitcast.3, s32[32,128]{1,0:T(8,128)} %bitcast.2, s32[2,64]{1,0:T(2,128)} %refs_5_.1, ...), custom_call_target="tpu_custom_call" | custom-call | tf_op jit(solution)/shard_map/evolver_backward/pallas_call | solution.py:679
  76.4 1.8 %hand_out.1 = (f32[256,128]{1,0:T(8,128)}, f32[3,256]{1,0:T(4,128)}, f32[128,128]{1,0:T(8,128)}, f32[128,128]{1,0:T(8,128)}, f32[4,128]{1,0:T(4,128)}, /*index=5*/f32[128,128]{1,0:T(8,128)}, f32[3,128]{1,0:T(4,128)}) custom-call(f32[256,128]{1,0:T(8,128)} %get-tuple-element.10.grad_x, f32[3,256]{1,0:T(4,128)} %get-tuple-element.11.grad_q, ...), custom_call_target="tpu_custom_call" | custom-call | tf_op jit(solution)/shard_map/hand_out/pallas_call | solution.py:741
